TPU v7x, 128 devices: a whole 4x4x4 slice. The times are simulated.
128 devices in a mesh: section: 4 (over y_hi, core), tensor: 8 (over y_lo, z), dp: 4 (over x).
Axes of the slice: x: 4, y: 4 (y_hi: 2, y_lo: 2; y = y_hi * 2 + y_lo), z: 4, core: 2. Of those that a mesh axis runs over, the one named last changes fastest.
Arguments:
- section_inputs: bfloat16 [4, 2, 512, 4096], P('section', None, ('dp', 'tensor')), may hold values from -100 to 100
- gain: float32 [4, 4096], P('section'), may hold values from 0.25 to 1.75
- w_gate: bfloat16 [4, 4096, 5120], P('section', None, 'tensor'), may hold values from -0.09375 to 0.09375
- w_up: bfloat16 [4, 4096, 5120], P('section', None, 'tensor'), may hold values from -0.09375 to 0.09375
- w_down: bfloat16 [4, 5120, 4096], P('section', 'tensor'), may hold values from -0.078125 to 0.078125
- cotangent: bfloat16 [2, 512, 4096], P(None, ('dp', 'tensor')), may hold values from -0.59765625 to 0.59765625
- lengths: int32 [2, 32], P(None, 'dp'), may hold values from 4 to 16, as said below
Outputs:
- grad_gate: bfloat16 [4, 4096, 5120], P('section', 'dp', 'tensor')
- grad_up: bfloat16 [4, 4096, 5120], P('section', 'dp', 'tensor')
- grad_down: bfloat16 [4, 5120, 4096], P('section', 'tensor', 'dp')
- grad_gain: float32 [4, 4096], P('section')
- grad_inputs: bfloat16 [4, 2, 512, 4096], P('section', None, ('dp', 'tensor'))
Inputs may be any that keep to these rules, and one draw needn't show every extreme that they name: `lengths`: each sequence's real tokens come first; the rest of its 16 positions are padding. Every micro-batch has a sequence without padding.
All inputs are finite; a program needn't handle non-finite values.
Results may differ from a plain program's by a relative error of at most 0.035.
Values may be sent and summed in bfloat16 or wider, within the bound.
A program may use at most 512 MiB of HBM per device.

v0:
```python
import math

import jax
import jax.numpy as jnp
from jax import lax
from jax.sharding import PartitionSpec as P

LEN = 16


EPSILON = 1e-06
GELU_SCALE = math.sqrt(2.0 / math.pi)
GELU_CUBIC = 0.044715
CONTRACT_ROWS = (((0,), (0,)), ((), ()))
CONTRACT_COLS = (((1,), (1,)), ((), ()))


def shifted(value, axis, steps):
    count = lax.axis_size(axis)
    first, last = (max(0, -steps), min(count, count - steps))
    return lax.ppermute(value, axis, [(source, source + steps) for source in range(first, last)])


def gelu_parts(pre_gate):
    tanh_arg = GELU_SCALE * (pre_gate + GELU_CUBIC * pre_gate * pre_gate * pre_gate)
    tanh_part = jnp.tanh(tanh_arg)
    gelu_value = 0.5 * pre_gate * (1.0 + tanh_part)
    gelu_slope = 0.5 * (1.0 + tanh_part) + 0.5 * pre_gate * (
        1.0 - tanh_part * tanh_part
    ) * GELU_SCALE * (1.0 + 3.0 * GELU_CUBIC * pre_gate * pre_gate)
    return (gelu_value, gelu_slope)


def pick_slot(stacked, slot_index):
    return lax.dynamic_index_in_dim(stacked, slot_index, 0, keepdims=False)


def store_slot(stacked, update, slot_index, active_flag):
    placed = lax.dynamic_update_index_in_dim(stacked, update, slot_index, 0)
    return jnp.where(active_flag, placed, stacked)


def hidden_grads(pre_gate, pre_up, upstream_full, down_here):
    grad_hidden = lax.dot_general(
        upstream_full, down_here, CONTRACT_COLS, preferred_element_type=jnp.float32
    )
    gelu_value, gelu_slope = gelu_parts(pre_gate)
    hidden = (gelu_value * pre_up).astype(jnp.bfloat16)
    grad_gate_in = (grad_hidden * pre_up * gelu_slope).astype(jnp.bfloat16)
    grad_up_in = (grad_hidden * gelu_value).astype(jnp.bfloat16)
    return (hidden, grad_gate_in, grad_up_in)


def weight_terms(normed_rows, upstream_rows, hidden_rows, gate_rows, up_rows):
    term_gate = lax.dot_general(
        normed_rows, gate_rows, CONTRACT_ROWS, preferred_element_type=jnp.float32
    )
    term_up = lax.dot_general(
        normed_rows, up_rows, CONTRACT_ROWS, preferred_element_type=jnp.float32
    )
    term_down = lax.dot_general(
        hidden_rows, upstream_rows, CONTRACT_ROWS, preferred_element_type=jnp.float32
    )
    return (term_gate, term_up, term_down)


def body(section_inputs, gain, w_gate, w_up, w_down, cotangent, lengths):
    section_count = lax.axis_size("section")
    section_id = lax.axis_index("section")
    inputs_here = section_inputs[0]
    gain_here = gain[0]
    gate_here = w_gate[0]
    up_here = w_up[0]
    down_here = w_down[0]
    micro_count, row_count, model_width = inputs_here.shape
    block_width = gate_here.shape[1]
    group_rows = row_count * lax.axis_size("tensor")
    token_ids = lax.axis_index("tensor") * row_count + jnp.arange(row_count, dtype=jnp.int32)
    owner_seq = token_ids // LEN
    position = token_ids % LEN
    seq_table = (
        owner_seq[:, None] == jnp.arange(lengths.shape[1], dtype=jnp.int32)[None, :]
    ).astype(jnp.int32)
    row_lengths = jnp.sum(seq_table[None, :, :] * lengths[:, None, :], axis=-1)
    keep_mask = (position[None, :] < row_lengths).astype(jnp.bfloat16)
    seeded = cotangent * keep_mask[:, :, None]
    inputs_float = inputs_here.astype(jnp.float32)
    inv_all = lax.rsqrt(jnp.mean(inputs_float * inputs_float, axis=-1, keepdims=True) + EPSILON)
    normed_all = (inputs_float * inv_all * gain_here).astype(jnp.bfloat16)
    zero_rows = jnp.zeros((row_count, model_width), jnp.bfloat16)
    outgoing = zero_rows
    grad_rows = jnp.zeros((micro_count, row_count, model_width), jnp.bfloat16)
    gain_term = jnp.zeros((model_width,), jnp.float32)
    keep_normed = jnp.zeros((micro_count, group_rows, model_width), jnp.bfloat16)
    keep_upstream = jnp.zeros((micro_count, group_rows, model_width), jnp.bfloat16)
    keep_hidden = jnp.zeros((micro_count, group_rows, block_width), jnp.bfloat16)
    keep_gate = jnp.zeros((micro_count, group_rows, block_width), jnp.bfloat16)
    keep_up = jnp.zeros((micro_count, group_rows, block_width), jnp.bfloat16)

    def spare_work(operands):
        zero_hidden = jnp.zeros((group_rows, block_width), jnp.bfloat16)
        return (zero_hidden, zero_hidden, zero_hidden)

    for step_number in range(micro_count + section_count - 1):
        slot_number = step_number - (section_count - 1) + section_id
        active_flag = jnp.logical_and(slot_number >= 0, slot_number < micro_count)
        slot_index = jnp.clip(slot_number, 0, micro_count - 1)
        if step_number == 0:
            arrived = zero_rows
        else:
            arrived = shifted(outgoing, "section", -1)
        upstream = jnp.where(
            section_id == section_count - 1, pick_slot(seeded, slot_index), arrived
        )
        rows_float = pick_slot(inputs_float, slot_index)
        inv_here = pick_slot(inv_all, slot_index)
        normed_full, upstream_full = (
            lax.all_gather(pick_slot(normed_all, slot_index), "tensor", axis=0, tiled=True),
            lax.all_gather(upstream, "tensor", axis=0, tiled=True),
        )
        operands = (normed_full, upstream_full)

        def local_work(operands):
            pre_gate = jnp.dot(operands[0], gate_here, preferred_element_type=jnp.float32)
            pre_up = jnp.dot(operands[0], up_here, preferred_element_type=jnp.float32)
            return hidden_grads(pre_gate, pre_up, operands[1], down_here)

        hidden, grad_gate_in, grad_up_in = lax.cond(active_flag, local_work, spare_work, operands)
        count = row_count * lax.axis_size("tensor")

        def compute(unused):
            total = lax.dot_general(
                grad_gate_in, gate_here, CONTRACT_COLS, preferred_element_type=jnp.float32
            )
            return total + lax.dot_general(
                grad_up_in, up_here, CONTRACT_COLS, preferred_element_type=jnp.float32
            )

        def skip_term(unused):
            return jnp.zeros((count, model_width), jnp.float32)

        grad_normed = lax.psum_scatter(
            lax.cond(active_flag, compute, skip_term, 0).astype(jnp.bfloat16),
            "tensor",
            scatter_dimension=0,
            tiled=True,
        ).astype(jnp.float32)
        scaled = grad_normed * gain_here
        result = (
            upstream.astype(jnp.float32)
            + inv_here * scaled
            - inv_here
            * inv_here
            * inv_here
            * rows_float
            * jnp.mean(scaled * rows_float, axis=-1, keepdims=True)
        )
        outgoing = result.astype(jnp.bfloat16)
        grad_rows = store_slot(grad_rows, outgoing, slot_index, active_flag)
        gain_term = gain_term + jnp.where(
            active_flag, jnp.sum(grad_normed * rows_float * inv_here, axis=0), 0.0
        )
        keep_normed = store_slot(keep_normed, normed_full, slot_index, active_flag)
        keep_upstream = store_slot(keep_upstream, upstream_full, slot_index, active_flag)
        keep_hidden = store_slot(keep_hidden, hidden, slot_index, active_flag)
        keep_gate = store_slot(keep_gate, grad_gate_in, slot_index, active_flag)
        keep_up = store_slot(keep_up, grad_up_in, slot_index, active_flag)
    weight_parts = weight_terms(
        keep_normed.reshape(-1, model_width),
        keep_upstream.reshape(-1, model_width),
        keep_hidden.reshape(-1, block_width),
        keep_gate.reshape(-1, block_width),
        keep_up.reshape(-1, block_width),
    )
    gate_sum, up_sum = (
        lax.psum_scatter(
            weight_parts[0].astype(jnp.bfloat16), "dp", scatter_dimension=0, tiled=True
        ).astype(jnp.float32),
        lax.psum_scatter(
            weight_parts[1].astype(jnp.bfloat16), "dp", scatter_dimension=0, tiled=True
        ).astype(jnp.float32),
    )
    down_sum = lax.psum_scatter(
        weight_parts[2].astype(jnp.bfloat16), "dp", scatter_dimension=1, tiled=True
    )
    gain_total = lax.psum(gain_term, ("tensor", "dp"))
    return (
        gate_sum.astype(jnp.bfloat16)[None],
        up_sum.astype(jnp.bfloat16)[None],
        down_sum[None],
        gain_total[None],
        grad_rows[None],
    )


def solution(mesh):
    in_specs = (
        P("section", None, ("dp", "tensor"), None),
        P("section", None),
        P("section", None, "tensor"),
        P("section", None, "tensor"),
        P("section", "tensor", None),
        P(None, ("dp", "tensor"), None),
        P(None, "dp"),
    )
    out_specs = (
        P("section", "dp", "tensor"),
        P("section", "dp", "tensor"),
        P("section", "tensor", "dp"),
        P("section", None),
        P("section", None, ("dp", "tensor"), None),
    )
    return jax.shard_map(body, mesh=mesh, in_specs=in_specs, out_specs=out_specs, check_vma=False)
```

profile of v0, /device:TPU:0, one launch (start us, length us, event | category | flops | bytes accessed | tf_op | source)
XLA Modules:
  0.0 865.8 jit_solution(16135971702843798614)
XLA Ops:
  13.0 38.9 %all-gather.35.cloned.1.call-done = bf16[1,128,4096]{2,1,0:T(8,128)(2,1)} async-done(((bf16[1,16,4096]{2,1,0:T(8,128)(2,1)}), bf16[1,128,4096]{2,1,0:T(8,128)(2,1)}) %all-gather.35.cloned.1.call-update) | async-done | bytes 1048592 | tf_op jit(solution)/shard_map/all_gather | solution.py:119
  51.9 40.5 %all-gather.25.cloned.1.call-done = bf16[1,128,4096]{2,1,0:T(8,128)(2,1)} async-done(((bf16[1,16,4096]{2,1,0:T(8,128)(2,1)}), bf16[1,128,4096]{2,1,0:T(8,128)(2,1)}) %all-gather.25.cloned.1.call-update) | async-done | bytes 1048592 | tf_op jit(solution)/shard_map/all_gather | solution.py:118
  96.8 46.3 %reduce-scatter.9.cloned.1.call-done = bf16[16,4096]{1,0:T(8,128)(2,1)} async-done(((bf16[128,4096]{1,0:T(8,128)(2,1)}), bf16[16,4096]{1,0:T(8,128)(2,1)}) %reduce-scatter.9.cloned.1.call-update) | async-done | bytes 131088 | tf_op jit(solution)/shard_map/reduce_scatter | solution.py:142
  149.3 33.1 %all-gather.27.cloned.1.call-done = bf16[1,128,4096]{2,1,0:T(8,128)(2,1)} async-done(((bf16[1,16,4096]{2,1,0:T(8,128)(2,1)}), bf16[1,128,4096]{2,1,0:T(8,128)(2,1)}) %all-gather.27.cloned.1.call-update) | async-done | bytes 1048592 | tf_op jit(solution)/shard_map/all_gather | solution.py:118
  182.4 39.7 %all-gather.17.cloned.1.call-done = bf16[128,4096]{1,0:T(8,128)(2,1)} async-done(((bf16[16,4096]{1,0:T(8,128)(2,1)}), bf16[128,4096]{1,0:T(8,128)(2,1)}) %all-gather.17.cloned.1.call-update) | async-done | bytes 1048592 | tf_op jit(solution)/shard_map/all_gather | solution.py:119
  226.6 52.5 %reduce-scatter.11.cloned.1.call-done = bf16[16,4096]{1,0:T(8,128)(2,1)} async-done(((bf16[128,4096]{1,0:T(8,128)(2,1)}), bf16[16,4096]{1,0:T(8,128)(2,1)}) %reduce-scatter.11.cloned.1.call-update) | async-done | bytes 131088 | tf_op jit(solution)/shard_map/reduce_scatter | solution.py:142
  285.3 33.2 %all-gather.29.cloned.1.call-done = bf16[1,128,4096]{2,1,0:T(8,128)(2,1)} async-done(((bf16[1,16,4096]{2,1,0:T(8,128)(2,1)}), bf16[1,128,4096]{2,1,0:T(8,128)(2,1)}) %all-gather.29.cloned.1.call-update) | async-done | bytes 1048592 | tf_op jit(solution)/shard_map/all_gather | solution.py:118
  318.5 39.9 %all-gather.19.cloned.1.call-done = bf16[128,4096]{1,0:T(8,128)(2,1)} async-done(((bf16[16,4096]{1,0:T(8,128)(2,1)}), bf16[128,4096]{1,0:T(8,128)(2,1)}) %all-gather.19.cloned.1.call-update) | async-done | bytes 1048592 | tf_op jit(solution)/shard_map/all_gather | solution.py:119
  362.3 52.7 %reduce-scatter.13.cloned.1.call-done = bf16[16,4096]{1,0:T(8,128)(2,1)} async-done(((bf16[128,4096]{1,0:T(8,128)(2,1)}), bf16[16,4096]{1,0:T(8,128)(2,1)}) %reduce-scatter.13.cloned.1.call-update) | async-done | bytes 131088 | tf_op jit(solution)/shard_map/reduce_scatter | solution.py:142
  421.1 33.0 %all-gather.31.cloned.1.call-done = bf16[1,128,4096]{2,1,0:T(8,128)(2,1)} async-done(((bf16[1,16,4096]{2,1,0:T(8,128)(2,1)}), bf16[1,128,4096]{2,1,0:T(8,128)(2,1)}) %all-gather.31.cloned.1.call-update) | async-done | bytes 1048592 | tf_op jit(solution)/shard_map/all_gather | solution.py:118
  454.2 39.9 %all-gather.21.cloned.1.call-done = bf16[128,4096]{1,0:T(8,128)(2,1)} async-done(((bf16[16,4096]{1,0:T(8,128)(2,1)}), bf16[128,4096]{1,0:T(8,128)(2,1)}) %all-gather.21.cloned.1.call-update) | async-done | bytes 1048592 | tf_op jit(solution)/shard_map/all_gather | solution.py:119
  494.1 9.2 %conditional.16 = (bf16[128,640]{1,0:T(8,128)(2,1)}, bf16[128,640]{1,0:T(8,128)(2,1)}, bf16[1,128,640]{2,1,0:T(8,128)(2,1)S(1)}, bf16[1,128,640]{2,1,0:T(8,128)(2,1)S(1)}) conditional(s32[]{:T(128)} %convert_element_type.177, () %tuple.110, (bf16[128,4096]{1,0:T(8,128)(2,1)}, bf16[640,4096]{1,0:T(8,128)(2,1)}, bf16[128,4096]{1,0:T(8,128)(2,1)}, ...), branch_computations={%region_20.21_spmd, %region_21.22_spmd} | conditional | flops 2015313920 | bytes 67141744 | solution.py:128
  494.1 4.7 fusion.126
  504.0 7.2 conditional.17
  504.0 4.5 fusion.128
  514.8 34.3 %reduce-scatter.15.cloned.1.call-done = bf16[16,4096]{1,0:T(8,128)(2,1)} async-done(((bf16[128,4096]{1,0:T(8,128)(2,1)}), bf16[16,4096]{1,0:T(8,128)(2,1)}) %reduce-scatter.15.cloned.1.call-update) | async-done | bytes 131088 | tf_op jit(solution)/shard_map/reduce_scatter | solution.py:142
  558.5 30.0 %all-gather.33.cloned.1.call-done = bf16[1,128,4096]{2,1,0:T(8,128)(2,1)} async-done(((bf16[1,16,4096]{2,1,0:T(8,128)(2,1)}), bf16[1,128,4096]{2,1,0:T(8,128)(2,1)}) %all-gather.33.cloned.1.call-update) | async-done | bytes 1048592 | tf_op jit(solution)/shard_map/all_gather | solution.py:118
  588.5 39.7 %all-gather.23.cloned.1.call-done = bf16[128,4096]{1,0:T(8,128)(2,1)} async-done(((bf16[16,4096]{1,0:T(8,128)(2,1)}), bf16[128,4096]{1,0:T(8,128)(2,1)}) %all-gather.23.cloned.1.call-update) | async-done | bytes 1048592 | tf_op jit(solution)/shard_map/all_gather | solution.py:119
  628.3 10.7 %conditional.18 = (bf16[128,640]{1,0:T(8,128)(2,1)}, bf16[128,640]{1,0:T(8,128)(2,1)}, bf16[1,128,640]{2,1,0:T(8,128)(2,1)}, bf16[1,128,640]{2,1,0:T(8,128)(2,1)}, bf16[1,128,640]{2,1,0:T(8,128)(2,1)S(1)}) conditional(s32[]{:T(128)} %convert_element_type.182, () %tuple.114, (bf16[128,4096]{1,0:T(8,128)(2,1)}, bf16[640,4096]{1,0:T(8,128)(2,1)}, ...), branch_computations={%region_26.27_spmd, %region_27.28_spmd} | conditional | flops 2015313920 | bytes 67469432 | solution.py:128
  628.3 4.7 fusion.129
  639.0 8.2 conditional.19
  674.5 9.6 %reduce-scatter.23.cloned.1.call-done = bf16[16,4096]{1,0:T(8,128)(2,1)} async-done(((bf16[128,4096]{1,0:T(8,128)(2,1)}), bf16[16,4096]{1,0:T(8,128)(2,1)}) %reduce-scatter.23.cloned.1.call-update) | async-done | bytes 131088 | tf_op jit(solution)/shard_map/reduce_scatter | solution.py:142
  685.3 159.2 %psum.7 = f32[1,4096]{1,0:T(1,128)} all-reduce(f32[1,4096]{1,0:T(1,128)S(1)} %bitcast.286), channel_id=1, replica_groups=mesh['section'=4,'tensor'=8,'dp'=4] {'tensor','dp'}, use_global_device_ids=true, to_apply=%region_39.40 | all-reduce | flops 4096 | bytes 32768 | tf_op jit(solution)/shard_map/psum | solution.py:186
  845.6 13.1 %reduce-scatter.17.cloned.1.call-done = bf16[1024,640]{1,0:T(8,128)(2,1)} async-done(((bf16[4096,640]{1,0:T(8,128)(2,1)}), bf16[1024,640]{1,0:T(8,128)(2,1)}) %reduce-scatter.17.cloned.1.call-update) | async-done | bytes 1310736 | tf_op jit(solution)/shard_map/reduce_scatter | solution.py:176
  (210 shorter events, 105.6 us)
Async XLA Ops:
  7.2 44.7 %all-gather.35.cloned.1.call-start = ((), (), s32[]{:S(2)}) async-start(), calls=%async_computation.25 | async-start | bytes 1179648 | tf_op jit(solution)/shard_map/all_gather | solution.py:119
  9.8 82.5 %all-gather.25.cloned.1.call-start = ((), (), s32[]{:S(2)}) async-start(), calls=%async_computation.20 | async-start | bytes 1179648 | tf_op jit(solution)/shard_map/all_gather | solution.py:118
  12.9 130.2 %reduce-scatter.9.cloned.1.call-start = ((), (), s32[]{:S(2)}) async-start(), calls=%async_computation.8 | async-start | bytes 1179648 | tf_op jit(solution)/shard_map/reduce_scatter | solution.py:142
  95.5 86.9 %all-gather.27.cloned.1.call-start = ((), (), s32[]{:S(2)}) async-start(), calls=%async_computation.21 | async-start | bytes 1179648 | tf_op jit(solution)/shard_map/all_gather | solution.py:118
  96.1 126.0 %all-gather.17.cloned.1.call-start = ((), (), s32[]{:S(2)}) async-start(), calls=%async_computation.9 | async-start | bytes 1179648 | tf_op jit(solution)/shard_map/all_gather | solution.py:119
  145.3 3.2 collective-permute-start
  149.2 129.8 %reduce-scatter.11.cloned.1.call-start = ((), (), s32[]{:S(2)}) async-start(), calls=%async_computation.10 | async-start | bytes 1179648 | tf_op jit(solution)/shard_map/reduce_scatter | solution.py:142
  225.8 92.7 %all-gather.29.cloned.1.call-start = ((), (), s32[]{:S(2)}) async-start(), calls=%async_computation.22 | async-start | bytes 1179648 | tf_op jit(solution)/shard_map/all_gather | solution.py:118
  226.6 131.8 %all-gather.19.cloned.1.call-start = ((), (), s32[]{:S(2)}) async-start(), calls=%async_computation.11 | async-start | bytes 1179648 | tf_op jit(solution)/shard_map/all_gather | solution.py:119
  281.3 3.2 collective-permute-start.1
  285.2 129.7 %reduce-scatter.13.cloned.1.call-start = ((), (), s32[]{:S(2)}) async-start(), calls=%async_computation.12 | async-start | bytes 1179648 | tf_op jit(solution)/shard_map/reduce_scatter | solution.py:142
  361.6 92.5 %all-gather.31.cloned.1.call-start = ((), (), s32[]{:S(2)}) async-start(), calls=%async_computation.23 | async-start | bytes 1179648 | tf_op jit(solution)/shard_map/all_gather | solution.py:118
  362.2 131.8 %all-gather.21.cloned.1.call-start = ((), (), s32[]{:S(2)}) async-start(), calls=%async_computation.13 | async-start | bytes 1179648 | tf_op jit(solution)/shard_map/all_gather | solution.py:119
  417.1 3.2 collective-permute-start.2
  421.1 128.0 %reduce-scatter.15.cloned.1.call-start = ((), (), s32[]{:S(2)}) async-start(), calls=%async_computation.14 | async-start | bytes 1179648 | tf_op jit(solution)/shard_map/reduce_scatter | solution.py:142
  512.2 76.3 %all-gather.33.cloned.1.call-start = ((), (), s32[]{:S(2)}) async-start(), calls=%async_computation.24 | async-start | bytes 1179648 | tf_op jit(solution)/shard_map/all_gather | solution.py:118
  513.0 115.3 %all-gather.23.cloned.1.call-start = ((), (), s32[]{:S(2)}) async-start(), calls=%async_computation.15 | async-start | bytes 1179648 | tf_op jit(solution)/shard_map/all_gather | solution.py:119
  551.4 3.2 collective-permute-start.3
  555.3 128.8 %reduce-scatter.23.cloned.1.call-start = ((), (), s32[]{:S(2)}) async-start(), calls=%async_computation.19 | async-start | bytes 1179648 | tf_op jit(solution)/shard_map/reduce_scatter | solution.py:142
  647.2 198.3 %reduce-scatter.21.cloned.1.call-start = ((), (), s32[]{:S(2)}) async-start(), calls=%async_computation.18 | async-start | bytes 6553600 | tf_op jit(solution)/shard_map/reduce_scatter | solution.py:183
  656.3 189.3 %reduce-scatter.19.cloned.1.call-start = ((), (), s32[]{:S(2)}) async-start(), calls=%async_computation.17 | async-start | bytes 6553600 | tf_op jit(solution)/shard_map/reduce_scatter | solution.py:179
  667.3 191.4 %reduce-scatter.17.cloned.1.call-start = ((), (), s32[]{:S(2)}) async-start(), calls=%async_computation.16 | async-start | bytes 6553600 | tf_op jit(solution)/shard_map/reduce_scatter | solution.py:176
  674.5 170.0 %copy-start.31 = (bf16[16,4096]{1,0:T(8,128)(2,1)S(1)}, bf16[16,4096]{1,0:T(8,128)(2,1)}, u32[]{:S(2)}) copy-start(bf16[16,4096]{1,0:T(8,128)(2,1)} %bitcast_select_fusion.10) | copy-start | bytes 393220
  674.5 170.0 %copy-start.44 = (f32[16]{0:T(128)S(1)}, f32[16]{0:T(128)}, u32[]{:S(2)}) copy-start(f32[16]{0:T(128)} %get-tuple-element.218) | copy-start | bytes 196
  (31 other events, 244.9 us)
Sparse Core Ops, SparseCore 0:
  10.2 41.6 all-gather.34
  54.1 38.1 all-gather.24
  95.6 47.4 reduce-scatter.8
  144.6 37.7 all-gather.26
  183.9 38.1 all-gather.16
  225.9 53.1 reduce-scatter.10
  280.7 37.7 all-gather.28
  320.1 38.1 all-gather.18
  361.7 53.1 reduce-scatter.12
  416.4 37.7 all-gather.30
  455.8 38.1 all-gather.20
  512.3 36.6 reduce-scatter.14
  550.7 37.7 all-gather.32
  590.0 38.1 all-gather.22
  647.3 36.7 reduce-scatter.22
  686.9 54.7 reduce-scatter.20
  744.6 55.9 reduce-scatter.18
  803.4 55.2 reduce-scatter.16
where the time goes:
time: 875 us; the launch traced here: 866 us
  waiting for transfers between devices  587 us (67%)
  blocking collectives  159 us (18%)
  matrix products  43 us (5%)
  other arithmetic  36.9 us (4%)
  local copies, waits for them, and re-layouts  18 us (2%)
  between operations  15 us (2%)
    all_gather x5, waiting for transfers between devices, body(): lax.all_gather(upstream, 'tensor', axis=0, tiled=True)  198 us
    reduce_scatter x5, waiting for transfers between devices, body(): lax.psum_scatter(lax.cond(active_flag, compute, skip_term, 0).astype(jnp....  195 us
    all_gather x5, waiting for transfers between devices, body(): lax.all_gather(pick_slot(normed_all, slot_index), 'tensor', axis=0, tiled...  170 us
    psum x1, blocking collectives, body(): gain_total = lax.psum(gain_term, ('tensor', 'dp'))  159 us
    select_n x30, other arithmetic, store_slot(): return jnp.where(active_flag, placed, stacked)  23.2 us
  transfers between devices with their start and end apart: 22, of which 20 were waited for; matrix products, arithmetic and copies ran while one was open for 6% of the time, Pallas kernels for 0%

commit v1 on v0

v1 whole, which is shorter than its diff:
```python
import functools
import math

import jax
import jax.numpy as jnp
from jax import lax
from jax.experimental import pallas as pl
from jax.experimental.pallas import tpu as pltpu
from jax.sharding import PartitionSpec as P

EPSILON = 1e-06
GELU_SCALE = math.sqrt(2.0 / math.pi)
GELU_CUBIC = 0.044715
MESH = pl.DeviceIdType.MESH
F32 = jnp.float32
BF16 = jnp.bfloat16
MICRO = 2
NN = (((1,), (0,)), ((), ()))
NT = (((1,), (1,)), ((), ()))
TN = (((0,), (0,)), ((), ()))


def dot(a, b, dims):
    return lax.dot_general(a, b, dims, preferred_element_type=F32)


def gelu_parts(pre_gate):
    tanh_arg = GELU_SCALE * (pre_gate + GELU_CUBIC * pre_gate * pre_gate * pre_gate)
    tanh_part = jnp.tanh(tanh_arg)
    gelu_value = 0.5 * pre_gate * (1.0 + tanh_part)
    gelu_slope = 0.5 * (1.0 + tanh_part) + 0.5 * pre_gate * (
        1.0 - tanh_part * tanh_part
    ) * GELU_SCALE * (1.0 + 3.0 * GELU_CUBIC * pre_gate * pre_gate)
    return (gelu_value, gelu_slope)


def kernel(
    dims,
    len_ref, x_ref, gain_ref, cot_ref, wg_hbm, wu_hbm, wd_hbm,
    og_ref, ou_ref, od_ref, ogain_ref, orow_ref,
    w2, wd, nbuf, ubuf, pbuf, rbuf, obuf, nslice, uslice, gall, hall, act, ups, inv_buf,
    gsum, gten, gdp_in, gdp,
    s_w, s_n, r_n, s_u, r_u, s_p, r_p, s_o, r_hop, s_x, r_x, s_gain, r_gain, go,
):
    T, C, R, F, CH = dims
    D = C * CH
    TOK = T * R
    s = lax.axis_index("section")
    t = lax.axis_index("tensor")
    d = lax.axis_index("dp")

    loads = [
        pltpu.make_async_copy(wg_hbm, w2.at[:, pl.ds(0, F)], s_w.at[0]),
        pltpu.make_async_copy(wu_hbm, w2.at[:, pl.ds(F, F)], s_w.at[1]),
        pltpu.make_async_copy(wd_hbm, wd, s_w.at[2]),
    ]
    for load in loads:
        load.start()

    def tpeer(k):
        return lax.rem(t + k, T)

    def dpeer(k):
        return lax.rem(d + k, C)

    barrier = pltpu.get_barrier_semaphore()

    def greet(where):
        pl.semaphore_signal(barrier, inc=1, device_id=where, device_id_type=MESH)

    for k in range(1, T):
        greet({"tensor": tpeer(k)})
    for k in range(1, C):
        greet({"dp": dpeer(k)})
    mate = s + 1 - 2 * lax.rem(s, 2)
    for k in range(T):
        greet({"section": mate, "tensor": lax.rem(t + k, T)})

    @pl.when(s == 1)
    def _():
        greet({"section": 2})

    @pl.when(s == 2)
    def _():
        greet({"section": 1})

    middle = jnp.where((s == 1) | (s == 2), 1, 0)
    pl.semaphore_wait(barrier, (T - 1) + (C - 1) + T + middle)

    def send(src, dst, ssem, rsem, where):
        pltpu.make_async_remote_copy(
            src_ref=src, dst_ref=dst, send_sem=ssem, recv_sem=rsem,
            device_id=where, device_id_type=MESH,
        ).start()

    def wait_for(ref, sem):
        pltpu.make_async_copy(ref, ref, sem).wait()

    def spread(buf, m, c, ssem, rsem):
        for k in range(1, T):
            send(buf.at[m, c, t], buf.at[m, c, t], ssem.at[m, c], rsem.at[m, c], {"tensor": tpeer(k)})

    def others(buf, m, c):
        return buf.at[m, c, pl.ds(0, T - 1)]

    keep_pos = lax.broadcasted_iota(jnp.int32, (R, 1), 0)
    for m in range(MICRO):
        square = jnp.zeros((R, 1), F32)
        for c in range(C):
            part = x_ref[m, :, c * CH : (c + 1) * CH].astype(F32)
            square += jnp.sum(part * part, axis=-1, keepdims=True)
        inv = lax.rsqrt(square * (1.0 / D) + EPSILON)
        inv_buf[m] = jnp.broadcast_to(inv, (R, 128))
        for c in range(C):
            cols = slice(c * CH, (c + 1) * CH)
            part = x_ref[m, :, cols].astype(F32)
            nbuf[m, c, t] = (part * inv * gain_ref[:, cols]).astype(BF16)

    @pl.when(s == 3)
    def _():
        for m in range(MICRO):
            keep = (keep_pos < len_ref[m, t]).astype(F32)
            for c in range(C):
                cols = slice(c * CH, (c + 1) * CH)
                ubuf[m, c, t] = (cot_ref[m, :, cols].astype(F32) * keep).astype(BF16)

    @pl.when(s == 2)
    def _():
        pl.semaphore_wait(go, 1)

    for c in range(C):
        spread(nbuf, 0, c, s_n, r_n)

    @pl.when(s == 3)
    def _():
        for c in range(C):
            spread(ubuf, 0, c, s_u, r_u)

    for load in loads:
        load.wait()

    def exchange_slices(buf, slices, which, m):
        for k in range(1, C):
            j = dpeer(k)
            send(buf.at[m, j], slices.at[m, d], s_x.at[m, which], r_x.at[m, which], {"dp": j})
        slices[m, d] = buf[m, d]

    def exchange_all(buf, which, m):
        for k in range(1, C):
            send(buf.at[m, d], buf.at[m, d], s_x.at[m, which], r_x.at[m, which], {"dp": dpeer(k)})

    def rows_of(buf, m, c):
        return buf[m, c].reshape(TOK, CH)

    def forward(m):
        total = jnp.zeros((TOK, 2 * F), F32)
        for c in range(C):
            total += dot(rows_of(nbuf, m, c), w2[c * CH : (c + 1) * CH, :], NN)
        pre_gate = total[:, :F]
        pre_up = total[:, F:]
        value, slope = gelu_parts(pre_gate)
        act[m] = value
        ups[m] = pre_up * slope
        hall[m, d] = (value * pre_up).astype(BF16)
        exchange_all(hall, 2, m)

    def wait_n(m):
        for c in range(C):
            wait_for(others(nbuf, m, c), r_n.at[m, c])

    wait_n(0)

    @pl.when(s < 3)
    def _():
        for c in range(C):
            spread(nbuf, 1, c, s_n, r_n)
    exchange_slices(nbuf, nslice, 0, 0)
    forward(0)

    @pl.when(s < 3)
    def _():
        wait_n(1)
        exchange_slices(nbuf, nslice, 0, 1)
        forward(1)

    def products(m):
        @pl.when(s == 1)
        def _():
            for c in range(C):
                wait_for(ubuf.at[m, c, t], r_hop.at[m, c])
                spread(ubuf, m, c, s_u, r_u)

        grad_hidden = jnp.zeros((TOK, F), F32)
        for c in range(C):
            @pl.when(lax.rem(s, 2) == 1)
            def _():
                wait_for(others(ubuf, m, c), r_u.at[m, c])

            @pl.when(lax.rem(s, 2) == 0)
            def _():
                wait_for(ubuf.at[m, c], r_u.at[m, c])
            grad_hidden += dot(rows_of(ubuf, m, c), wd[:, c * CH : (c + 1) * CH], NT)
        if m == 0:
            @pl.when(s == 3)
            def _():
                pl.semaphore_signal(go, inc=1, device_id={"section": mate}, device_id_type=MESH)
        gall[m, d, :, :F] = (grad_hidden * ups[m]).astype(BF16)
        gall[m, d, :, F:] = (grad_hidden * act[m]).astype(BF16)
        both = gall[m, d]
        for c in range(C):
            term = dot(both, w2[c * CH : (c + 1) * CH, :], NT).astype(BF16)
            pbuf[m, c] = term.reshape(T, R, CH)
            rbuf[m, c, t] = pbuf[m, c, t]
            for k in range(1, T):
                j = tpeer(k)
                send(pbuf.at[m, c, j], rbuf.at[m, c, t], s_p.at[m, c], r_p.at[m, c], {"tensor": j})
        exchange_all(gall, 3, m)
        exchange_slices(ubuf, uslice, 1, m)

    def finish(m):
        inv = inv_buf[m, :, 0:1]
        mean = jnp.zeros((R, 1), F32)
        sums = []
        for c in range(C):
            cols = slice(c * CH, (c + 1) * CH)
            wait_for(others(rbuf, m, c), r_p.at[m, c])
            grad_normed = jnp.zeros((R, CH), F32)
            for j in range(T):
                grad_normed += rbuf[m, c, j].astype(F32)
            part = x_ref[m, :, cols].astype(F32)
            scaled = grad_normed * gain_ref[:, cols]
            mean += jnp.sum(scaled * part, axis=-1, keepdims=True)
            gain_part = jnp.sum(grad_normed * part * inv, axis=0, keepdims=True)
            if m == 0:
                gsum[:, cols] = gain_part
            else:
                gsum[:, cols] += gain_part
            sums.append(scaled)
        factor = inv * inv * inv * (mean * (1.0 / D))
        for c in range(C):
            cols = slice(c * CH, (c + 1) * CH)
            part = x_ref[m, :, cols].astype(F32)
            result = ubuf[m, c, t].astype(F32) + inv * sums[c] - part * factor
            rows = result.astype(BF16)
            obuf[m, c] = rows
            orow_ref[m, :, cols] = rows

            @pl.when(lax.rem(s, 2) == 1)
            def _():
                for k in range(T):
                    send(obuf.at[m, c], ubuf.at[m, c, t], s_o.at[m, c], r_u.at[m, c],
                         {"section": s - 1, "tensor": lax.rem(t + k, T)})

            @pl.when(s == 2)
            def _():
                send(obuf.at[m, c], ubuf.at[m, c, t], s_o.at[m, c], r_hop.at[m, c], {"section": s - 1})

    products(0)

    @pl.when(s == 3)
    def _():
        for c in range(C):
            spread(nbuf, 1, c, s_n, r_n)
        for c in range(C):
            spread(ubuf, 1, c, s_u, r_u)
        wait_n(1)
        exchange_slices(nbuf, nslice, 0, 1)
        forward(1)

    finish(0)
    products(1)
    finish(1)

    gten[t] = gsum[...]
    for k in range(1, T):
        send(gsum, gten.at[t], s_gain.at[0], r_gain.at[0], {"tensor": tpeer(k)})

    for m in range(MICRO):
        wait_for(nslice.at[m, pl.ds(0, C - 1)], r_x.at[m, 0])
        wait_for(uslice.at[m, pl.ds(0, C - 1)], r_x.at[m, 1])
        wait_for(hall.at[m, pl.ds(0, C - 1)], r_x.at[m, 2])
        wait_for(gall.at[m, pl.ds(0, C - 1)], r_x.at[m, 3])

    count = MICRO * C * TOK
    grads = gall[...].reshape(count, 2 * F)
    step = min(256, CH)
    for n in range(CH // step):
        rows = slice(n * step, (n + 1) * step)
        left = nslice[:, :, :, :, rows].reshape(count, step)
        term = dot(left, grads, TN)
        og_ref[rows, :] = term[:, :F].astype(BF16)
        ou_ref[rows, :] = term[:, F:].astype(BF16)

    wait_for(gten.at[pl.ds(0, T - 1)], r_gain.at[0])
    gain_total = gten[0]
    for j in range(1, T):
        gain_total += gten[j]
    gdp_in[...] = gain_total
    gdp[d] = gain_total
    for k in range(1, C):
        send(gdp_in, gdp.at[d], s_gain.at[1], r_gain.at[1], {"dp": dpeer(k)})

    hidden = hall[...].reshape(count, F)
    for n in range(CH // step):
        cols = slice(n * step, (n + 1) * step)
        right = uslice[:, :, :, :, cols].reshape(count, step)
        od_ref[:, cols] = dot(hidden, right, TN).astype(BF16)

    wait_for(gdp.at[pl.ds(0, C - 1)], r_gain.at[1])
    gain_total = gdp[0]
    for j in range(1, C):
        gain_total += gdp[j]
    ogain_ref[...] = gain_total

    for m in range(MICRO):
        for c in range(C):
            wait_for(others(nbuf, m, c), s_n.at[m, c])
            wait_for(others(pbuf, m, c), s_p.at[m, c])

            @pl.when(lax.rem(s, 2) == 1)
            def _():
                wait_for(others(ubuf, m, c), s_u.at[m, c])
                wait_for(ubuf.at[m, c], s_o.at[m, c])

            @pl.when(s == 2)
            def _():
                wait_for(obuf.at[m, c], s_o.at[m, c])
        wait_for(nslice.at[m, pl.ds(0, C - 1)], s_x.at[m, 0])
        wait_for(uslice.at[m, pl.ds(0, C - 1)], s_x.at[m, 1])
        wait_for(hall.at[m, pl.ds(0, C - 1)], s_x.at[m, 2])
        wait_for(gall.at[m, pl.ds(0, C - 1)], s_x.at[m, 3])
    wait_for(gten.at[pl.ds(0, T - 1)], s_gain.at[0])
    wait_for(gdp.at[pl.ds(0, C - 1)], s_gain.at[1])


def body(T, C, section_inputs, gain, w_gate, w_up, w_down, cotangent, lengths):
    _, micro, R, D = section_inputs.shape
    F = w_gate.shape[2]
    CH = D // C
    TOK = T * R
    dims = (T, C, R, F, CH)
    vmem = pl.BlockSpec(memory_space=pltpu.VMEM)
    smem = pl.BlockSpec(memory_space=pltpu.SMEM)
    hbm = pl.BlockSpec(memory_space=pl.ANY)
    dma = pltpu.SemaphoreType.DMA
    flops = 2 * micro * 8 * TOK * D * F
    outs = pl.pallas_call(
        functools.partial(kernel, dims),
        out_shape=(
            jax.ShapeDtypeStruct((CH, F), BF16),
            jax.ShapeDtypeStruct((CH, F), BF16),
            jax.ShapeDtypeStruct((F, CH), BF16),
            jax.ShapeDtypeStruct((1, D), F32),
            jax.ShapeDtypeStruct((micro, R, D), BF16),
        ),
        in_specs=[smem, vmem, vmem, vmem, hbm, hbm, hbm],
        out_specs=(vmem, vmem, vmem, vmem, vmem),
        scratch_shapes=[
            pltpu.VMEM((D, 2 * F), BF16),
            pltpu.VMEM((F, D), BF16),
            pltpu.VMEM((micro, C, T, R, CH), BF16),
            pltpu.VMEM((micro, C, T, R, CH), BF16),
            pltpu.VMEM((micro, C, T, R, CH), BF16),
            pltpu.VMEM((micro, C, T, R, CH), BF16),
            pltpu.VMEM((micro, C, R, CH), BF16),
            pltpu.VMEM((micro, C, T, R, CH), BF16),
            pltpu.VMEM((micro, C, T, R, CH), BF16),
            pltpu.VMEM((micro, C, TOK, 2 * F), BF16),
            pltpu.VMEM((micro, C, TOK, F), BF16),
            pltpu.VMEM((micro, TOK, F), F32),
            pltpu.VMEM((micro, TOK, F), F32),
            pltpu.VMEM((micro, R, 128), F32),
            pltpu.VMEM((1, D), F32),
            pltpu.VMEM((T, 1, D), F32),
            pltpu.VMEM((1, D), F32),
            pltpu.VMEM((C, 1, D), F32),
            dma((3,)),
            dma((micro, C)),
            dma((micro, C)),
            dma((micro, C)),
            dma((micro, C)),
            dma((micro, C)),
            dma((micro, C)),
            dma((micro, C)),
            dma((micro, C)),
            dma((micro, 4)),
            dma((micro, 4)),
            dma((2,)),
            dma((2,)),
            pltpu.SemaphoreType.REGULAR,
        ],
        cost_estimate=pl.CostEstimate(
            flops=flops, bytes_accessed=24 * D * F // 2, transcendentals=micro * TOK * F
        ),
        compiler_params=pltpu.CompilerParams(
            collective_id=0, has_side_effects=True, vmem_limit_bytes=60 * 1024 * 1024
        ),
    )(lengths, section_inputs[0], gain, cotangent, w_gate[0], w_up[0], w_down[0])
    gate, up, down, gain_out, rows = outs
    return (gate[None], up[None], down[None], gain_out, rows[None])


def solution(mesh):
    T, C = mesh.shape["tensor"], mesh.shape["dp"]
    in_specs = (
        P("section", None, ("dp", "tensor"), None),
        P("section", None),
        P("section", None, "tensor"),
        P("section", None, "tensor"),
        P("section", "tensor", None),
        P(None, ("dp", "tensor"), None),
        P(None, "dp"),
    )
    out_specs = (
        P("section", "dp", "tensor"),
        P("section", "dp", "tensor"),
        P("section", "tensor", "dp"),
        P("section", None),
        P("section", None, ("dp", "tensor"), None),
    )
    return jax.shard_map(
        functools.partial(body, T, C), mesh=mesh, in_specs=in_specs, out_specs=out_specs, check_vma=False
    )
```

time: 875 us -> 169 us (0.19)
  waiting for transfers between devices: 587 us -> 0 us
  Pallas kernels: 0 us -> 161 us
  blocking collectives: 159 us -> 0 us
  matrix products: 43 us -> 0 us
  other arithmetic: 36.9 us -> 0 us
  between operations: 15 us -> 0.66 us
  local copies, waits for them, and re-layouts: 18 us -> 6.75 us
    all_gather x10 -> x0, waiting for transfers between devices: 368 us -> none  [the longest x5 198 us: body(): lax.all_gather(upstream, 'tensor', axis=0, tiled=True)]
    reduce_scatter x8 -> x0, waiting for transfers between devices: 208 us -> none  [the longest x5 195 us: body(): lax.psum_scatter(lax.cond(active_flag, compute, skip_term, 0).astype(jnp....]
    pallas_call x0 -> x1, Pallas kernels: none -> 161 us  [body(): pl.pallas_call(functools.partial(kernel, dims), out_shape=(jax.ShapeDtype...]
    psum x1 -> x0, blocking collectives: 159 us -> none  [body(): gain_total = lax.psum(gain_term, ('tensor', 'dp'))]
    dot_general x13 -> x0, matrix products: 43 us -> none  [the longest x2 9.39 us: hidden_grads(): lax.dot_general(upstream_full, down_here, CONTRACT_COLS, preferred_elemen...]
    select_n x36 -> x0, other arithmetic: 26.6 us -> none  [the longest x30 23.2 us: store_slot(): return jnp.where(active_flag, placed, stacked)]
  transfers between devices with their start and end apart: 22 -> 0, of which waited for: 20 -> 0; matrix products, arithmetic and copies ran while one was open for 6% -> 0% of each run, Pallas kernels for 0% -> 0%
where the time goes in v1:
time: 169 us; the launch traced here: 168 us
  Pallas kernels  161 us (95%)
  local copies, waits for them, and re-layouts  6.75 us (4%)
    pallas_call x1, Pallas kernels, body(): pl.pallas_call(functools.partial(kernel, dims), out_shape=(jax.ShapeDtype...  161 us
    unnamed x13, local copies, waits for them, and re-layouts  6.75 us

profile of v1, /device:TPU:0, one launch (start us, length us, event | category | flops | bytes accessed | tf_op | source)
XLA Modules:
  0.0 168.3 jit_solution(12030747254585957892)
XLA Ops:
  0.6 160.9 %shard_map.110 = (bf16[1024,640]{1,0:T(8,128)(2,1)}, bf16[1024,640]{1,0:T(8,128)(2,1)}, bf16[640,1024]{1,0:T(8,128)(2,1)}, f32[1,4096]{1,0:T(1,128)}, bf16[2,16,4096]{2,1,0:T(8,128)(2,1)}) custom-call(s32[2,8]{1,0:T(2,128)} %len_ref.1, bf16[2,16,4096]{2,1,0:T(8,128)(2,1)} %bitcast.15, f32[1,4096]{1,0:T(1,128)} %gain_ref.1, bf16[2,16,4096]{2,1,0:T(8,128)(2,1)} %cot_ref.1, ...), custom_call_target="tpu_custom_call" | custom-call | flops 10737418240 | bytes 31457280 | tf_op jit(solution)/shard_map/pallas_call | solution.py:347
  161.6 0.0 copy-start.1
  161.6 2.6 %copy.17 = bf16[1,1024,640]{2,1,0:T(8,128)(2,1)} copy(bf16[1,1024,640]{2,1,0:T(8,128)(2,1)} %bitcast.10) | data formatting | bytes 2621440
  164.2 0.0 copy-done.1
  164.2 0.0 copy-start
  164.2 1.1 copy.18
  165.2 0.7 copy-done
  166.0 0.0 copy-start.3
  166.0 0.0 copy-start.2
  166.0 1.1 copy.19
  167.0 0.0 copy-done.3
  167.0 0.6 copy.20
  167.6 0.0 copy-done.2
  167.6 0.7 copy.21
Async XLA Ops:
  161.6 2.6 %copy-start.1 = (bf16[1024,640]{1,0:T(8,128)(2,1)S(1)}, bf16[1024,640]{1,0:T(8,128)(2,1)}, u32[]{:S(2)}) copy-start(bf16[1024,640]{1,0:T(8,128)(2,1)} %get-tuple-element.11) | copy-start | bytes 3932164
  164.2 1.8 %copy-start = (bf16[640,1024]{1,0:T(8,128)(2,1)S(1)}, bf16[640,1024]{1,0:T(8,128)(2,1)}, u32[]{:S(2)}) copy-start(bf16[640,1024]{1,0:T(8,128)(2,1)} %get-tuple-element.12) | copy-start | bytes 3932164
  166.0 1.1 copy-start.3
  166.0 1.7 copy-start.2

commit v2 on v1

--- a/solution.py
+++ b/solution.py
@@ -38,13 +38,14 @@
     dims,
     len_ref, x_ref, gain_ref, cot_ref, wg_hbm, wu_hbm, wd_hbm,
     og_ref, ou_ref, od_ref, ogain_ref, orow_ref,
-    w2, wd, nbuf, ubuf, pbuf, rbuf, obuf, nslice, uslice, gall, hall, act, ups, inv_buf,
-    gsum, gten, gdp_in, gdp,
-    s_w, s_n, r_n, s_u, r_u, s_p, r_p, s_o, r_hop, s_x, r_x, s_gain, r_gain, go,
+    w2, wd, nbuf, ubuf, pbuf, rbuf, obuf, nstage, relay, nslice, uslice, gall, hall, act, ups, inv_buf,
+    accg, accd, gsum, gten, gdp_in, gdp,
+    s_w, s_n, r_n, s_u, r_u, s_p, r_p, s_o, r_hop, s_l, r_l, s_f, s_x, r_x, s_gain, r_gain, go,
 ):
     T, C, R, F, CH = dims
     D = C * CH
     TOK = T * R
+    HALF = T // 2
     s = lax.axis_index("section")
     t = lax.axis_index("tensor")
     d = lax.axis_index("dp")
@@ -84,8 +85,20 @@
     def _():
         greet({"section": 1})
 
+    cross = lax.rem(s + 2, 4)
+    facing = lax.rem(t + HALF, T)
+    odd = lax.rem(s, 2) == 1
+
+    @pl.when(odd)
+    def _():
+        greet({"section": cross, "tensor": facing})
+
+    @pl.when(jnp.logical_not(odd))
+    def _():
+        for k in range(T):
+            greet({"section": cross, "tensor": lax.rem(t + k, T)})
+
     middle = jnp.where((s == 1) | (s == 2), 1, 0)
-    pl.semaphore_wait(barrier, (T - 1) + (C - 1) + T + middle)
 
     def send(src, dst, ssem, rsem, where):
         pltpu.make_async_remote_copy(
@@ -113,28 +126,89 @@
         inv_buf[m] = jnp.broadcast_to(inv, (R, 128))
         for c in range(C):
             cols = slice(c * CH, (c + 1) * CH)
-            part = x_ref[m, :, cols].astype(F32)
-            nbuf[m, c, t] = (part * inv * gain_ref[:, cols]).astype(BF16)
+            rows = (x_ref[m, :, cols].astype(F32) * inv * gain_ref[:, cols]).astype(BF16)
+            nstage[m, c] = rows
+
+            @pl.when(s != 2)
+            def _():
+                nbuf[m, c, t] = rows
+
+    def seeds(m, c):
+        keep = (keep_pos < len_ref[m, t]).astype(F32)
+        return (cot_ref[m, :, c * CH : (c + 1) * CH].astype(F32) * keep).astype(BF16)
+
+    row = (t // HALF) * HALF
+
+    def rowpeer(k):
+        return row + lax.rem(t - row + k, HALF)
+
+    def spread_row(buf, m, c, ssem, rsem):
+        for k in range(1, HALF):
+            send(buf.at[m, c, t], buf.at[m, c, t], ssem.at[m, c], rsem.at[m, c], {"tensor": rowpeer(k)})
+
+    def send_seeds(m):
+        for c in range(C):
+            spread_row(ubuf, m, c, s_u, r_u)
 
     @pl.when(s == 3)
     def _():
         for m in range(MICRO):
-            keep = (keep_pos < len_ref[m, t]).astype(F32)
-            for c in range(C):
-                cols = slice(c * CH, (c + 1) * CH)
-                ubuf[m, c, t] = (cot_ref[m, :, cols].astype(F32) * keep).astype(BF16)
+            for c in range(C):
+                ubuf[m, c, t] = seeds(m, c)
+
+    @pl.when(s == 1)
+    def _():
+        for m in range(MICRO):
+            for c in range(C):
+                relay[m, c, t] = seeds(m, c)
+
+    pl.semaphore_wait(barrier, (T - 1) + (C - 1) + T + middle + jnp.where(odd, 1, T))
+    @pl.when(s == 3)
+    def _():
+        for c in range(C):
+            spread(nbuf, 0, c, s_n, r_n)
+        send_seeds(0)
+
+    @pl.when(s == 1)
+    def _():
+        for m in range(MICRO):
+            for c in range(C):
+                spread_row(relay, m, c, s_l, r_l)
+        for m in range(MICRO):
+            for c in range(C):
+                wait_for(relay.at[m, c, pl.ds(0, HALF - 1)], r_l.at[m, c])
+                part = pl.ds(row, HALF)
+                send(relay.at[m, c, part], ubuf.at[m, c, part], s_f.at[m, c], r_u.at[m, c],
+                     {"section": cross, "tensor": facing})
+            for c in range(C):
+                wait_for(relay.at[m, c, pl.ds(0, HALF)], s_f.at[m, c])
+            if m == 0:
+                pl.semaphore_signal(go, inc=1, device_id={"section": mate}, device_id_type=MESH)
 
     @pl.when(s == 2)
     def _():
+        for m in range(MICRO):
+            for c in range(C):
+                for k in range(T):
+                    send(nstage.at[m, c], relay.at[m, c, t], s_l.at[m, c], r_l.at[m, c],
+                         {"section": cross, "tensor": lax.rem(t + k, T)})
+
+    @pl.when(s == 0)
+    def _():
         pl.semaphore_wait(go, 1)
-
-    for c in range(C):
-        spread(nbuf, 0, c, s_n, r_n)
-
-    @pl.when(s == 3)
-    def _():
-        for c in range(C):
-            spread(ubuf, 0, c, s_u, r_u)
+        for m in range(MICRO):
+            for c in range(C):
+                wait_for(relay.at[m, c], r_l.at[m, c])
+                send(relay.at[m, c], nbuf.at[m, c], s_f.at[m, c], r_n.at[m, c],
+                     {"section": cross, "tensor": facing})
+            for c in range(C):
+                wait_for(relay.at[m, c], s_f.at[m, c])
+
+    @pl.when(s < 2)
+    def _():
+        for m in range(MICRO):
+            for c in range(C):
+                spread(nbuf, m, c, s_n, r_n)
 
     for load in loads:
         load.wait()
@@ -166,18 +240,19 @@
 
     def wait_n(m):
         for c in range(C):
-            wait_for(others(nbuf, m, c), r_n.at[m, c])
+            @pl.when(s == 2)
+            def _():
+                wait_for(nbuf.at[m, c], r_n.at[m, c])
+
+            @pl.when(s != 2)
+            def _():
+                wait_for(others(nbuf, m, c), r_n.at[m, c])
 
     wait_n(0)
-
-    @pl.when(s < 3)
-    def _():
-        for c in range(C):
-            spread(nbuf, 1, c, s_n, r_n)
+    forward(0)
     exchange_slices(nbuf, nslice, 0, 0)
-    forward(0)
-
-    @pl.when(s < 3)
+
+    @pl.when(s < 2)
     def _():
         wait_n(1)
         exchange_slices(nbuf, nslice, 0, 1)
@@ -192,20 +267,18 @@
 
         grad_hidden = jnp.zeros((TOK, F), F32)
         for c in range(C):
-            @pl.when(lax.rem(s, 2) == 1)
+            @pl.when(odd)
             def _():
                 wait_for(others(ubuf, m, c), r_u.at[m, c])
 
-            @pl.when(lax.rem(s, 2) == 0)
+            @pl.when(jnp.logical_not(odd))
             def _():
                 wait_for(ubuf.at[m, c], r_u.at[m, c])
             grad_hidden += dot(rows_of(ubuf, m, c), wd[:, c * CH : (c + 1) * CH], NT)
-        if m == 0:
-            @pl.when(s == 3)
-            def _():
-                pl.semaphore_signal(go, inc=1, device_id={"section": mate}, device_id_type=MESH)
+        exchange_slices(ubuf, uslice, 1, m)
         gall[m, d, :, :F] = (grad_hidden * ups[m]).astype(BF16)
         gall[m, d, :, F:] = (grad_hidden * act[m]).astype(BF16)
+        exchange_all(gall, 3, m)
         both = gall[m, d]
         for c in range(C):
             term = dot(both, w2[c * CH : (c + 1) * CH, :], NT).astype(BF16)
@@ -214,8 +287,12 @@
             for k in range(1, T):
                 j = tpeer(k)
                 send(pbuf.at[m, c, j], rbuf.at[m, c, t], s_p.at[m, c], r_p.at[m, c], {"tensor": j})
-        exchange_all(gall, 3, m)
-        exchange_slices(ubuf, uslice, 1, m)
+        if m == 0:
+            @pl.when(s == 3)
+            def _():
+                for c in range(C):
+                    spread(nbuf, 1, c, s_n, r_n)
+                send_seeds(1)
 
     def finish(m):
         inv = inv_buf[m, :, 0:1]
@@ -245,7 +322,7 @@
             obuf[m, c] = rows
             orow_ref[m, :, cols] = rows
 
-            @pl.when(lax.rem(s, 2) == 1)
+            @pl.when(odd)
             def _():
                 for k in range(T):
                     send(obuf.at[m, c], ubuf.at[m, c, t], s_o.at[m, c], r_u.at[m, c],
@@ -256,40 +333,52 @@
                 send(obuf.at[m, c], ubuf.at[m, c, t], s_o.at[m, c], r_hop.at[m, c], {"section": s - 1})
 
     products(0)
-
-    @pl.when(s == 3)
-    def _():
-        for c in range(C):
-            spread(nbuf, 1, c, s_n, r_n)
-        for c in range(C):
-            spread(ubuf, 1, c, s_u, r_u)
+    finish(0)
+
+    @pl.when(s >= 2)
+    def _():
         wait_n(1)
+        forward(1)
         exchange_slices(nbuf, nslice, 0, 1)
-        forward(1)
-
-    finish(0)
+
     products(1)
-    finish(1)
-
-    gten[t] = gsum[...]
-    for k in range(1, T):
-        send(gsum, gten.at[t], s_gain.at[0], r_gain.at[0], {"tensor": tpeer(k)})
-
-    for m in range(MICRO):
+
+    count = C * TOK
+    step = min(256, CH)
+
+    def arrived(m):
         wait_for(nslice.at[m, pl.ds(0, C - 1)], r_x.at[m, 0])
         wait_for(uslice.at[m, pl.ds(0, C - 1)], r_x.at[m, 1])
         wait_for(hall.at[m, pl.ds(0, C - 1)], r_x.at[m, 2])
         wait_for(gall.at[m, pl.ds(0, C - 1)], r_x.at[m, 3])
 
-    count = MICRO * C * TOK
-    grads = gall[...].reshape(count, 2 * F)
-    step = min(256, CH)
+    def term_gate_up(m, rows):
+        return dot(nslice[m, :, :, :, rows].reshape(count, step), gall[m].reshape(count, 2 * F), TN)
+
+    def term_down(m, cols):
+        return dot(hall[m].reshape(count, F), uslice[m, :, :, :, cols].reshape(count, step), TN)
+
+    def first_terms():
+        arrived(0)
+        for n in range(CH // step):
+            part = slice(n * step, (n + 1) * step)
+            accg[part, :] = term_gate_up(0, part)
+            accd[:, part] = term_down(0, part)
+
+    pl.when(s == 0)(first_terms)
+    finish(1)
+
+    gten[t] = gsum[...]
+    for k in range(1, T):
+        send(gsum, gten.at[t], s_gain.at[0], r_gain.at[0], {"tensor": tpeer(k)})
+
+    pl.when(s > 0)(first_terms)
+    arrived(1)
     for n in range(CH // step):
         rows = slice(n * step, (n + 1) * step)
-        left = nslice[:, :, :, :, rows].reshape(count, step)
-        term = dot(left, grads, TN)
-        og_ref[rows, :] = term[:, :F].astype(BF16)
-        ou_ref[rows, :] = term[:, F:].astype(BF16)
+        total = accg[rows, :] + term_gate_up(1, rows)
+        og_ref[rows, :] = total[:, :F].astype(BF16)
+        ou_ref[rows, :] = total[:, F:].astype(BF16)
 
     wait_for(gten.at[pl.ds(0, T - 1)], r_gain.at[0])
     gain_total = gten[0]
@@ -300,11 +389,9 @@
     for k in range(1, C):
         send(gdp_in, gdp.at[d], s_gain.at[1], r_gain.at[1], {"dp": dpeer(k)})
 
-    hidden = hall[...].reshape(count, F)
     for n in range(CH // step):
         cols = slice(n * step, (n + 1) * step)
-        right = uslice[:, :, :, :, cols].reshape(count, step)
-        od_ref[:, cols] = dot(hidden, right, TN).astype(BF16)
+        od_ref[:, cols] = (accd[:, cols] + term_down(1, cols)).astype(BF16)
 
     wait_for(gdp.at[pl.ds(0, C - 1)], r_gain.at[1])
     gain_total = gdp[0]
@@ -314,16 +401,28 @@
 
     for m in range(MICRO):
         for c in range(C):
-            wait_for(others(nbuf, m, c), s_n.at[m, c])
             wait_for(others(pbuf, m, c), s_p.at[m, c])
 
-            @pl.when(lax.rem(s, 2) == 1)
-            def _():
+            @pl.when(odd)
+            def _():
+                wait_for(ubuf.at[m, c], s_o.at[m, c])
+
+            @pl.when(s == 1)
+            def _():
+                wait_for(relay.at[m, c, pl.ds(0, HALF - 1)], s_l.at[m, c])
                 wait_for(others(ubuf, m, c), s_u.at[m, c])
-                wait_for(ubuf.at[m, c], s_o.at[m, c])
+
+            @pl.when(s == 3)
+            def _():
+                wait_for(ubuf.at[m, c, pl.ds(0, HALF - 1)], s_u.at[m, c])
+
+            @pl.when(s != 2)
+            def _():
+                wait_for(others(nbuf, m, c), s_n.at[m, c])
 
             @pl.when(s == 2)
             def _():
+                wait_for(relay.at[m, c], s_l.at[m, c])
                 wait_for(obuf.at[m, c], s_o.at[m, c])
         wait_for(nslice.at[m, pl.ds(0, C - 1)], s_x.at[m, 0])
         wait_for(uslice.at[m, pl.ds(0, C - 1)], s_x.at[m, 1])
@@ -347,11 +446,11 @@
     outs = pl.pallas_call(
         functools.partial(kernel, dims),
         out_shape=(
-            jax.ShapeDtypeStruct((CH, F), BF16),
-            jax.ShapeDtypeStruct((CH, F), BF16),
-            jax.ShapeDtypeStruct((F, CH), BF16),
-            jax.ShapeDtypeStruct((1, D), F32),
-            jax.ShapeDtypeStruct((micro, R, D), BF16),
+            pltpu.VMEM((CH, F), BF16),
+            pltpu.VMEM((CH, F), BF16),
+            pltpu.VMEM((F, CH), BF16),
+            pltpu.VMEM((1, D), F32),
+            pltpu.VMEM((micro, R, D), BF16),
         ),
         in_specs=[smem, vmem, vmem, vmem, hbm, hbm, hbm],
         out_specs=(vmem, vmem, vmem, vmem, vmem),
@@ -363,6 +462,8 @@
             pltpu.VMEM((micro, C, T, R, CH), BF16),
             pltpu.VMEM((micro, C, T, R, CH), BF16),
             pltpu.VMEM((micro, C, R, CH), BF16),
+            pltpu.VMEM((micro, C, R, CH), BF16),
+            pltpu.VMEM((micro, C, T, R, CH), BF16),
             pltpu.VMEM((micro, C, T, R, CH), BF16),
             pltpu.VMEM((micro, C, T, R, CH), BF16),
             pltpu.VMEM((micro, C, TOK, 2 * F), BF16),
@@ -370,11 +471,16 @@
             pltpu.VMEM((micro, TOK, F), F32),
             pltpu.VMEM((micro, TOK, F), F32),
             pltpu.VMEM((micro, R, 128), F32),
+            pltpu.VMEM((CH, 2 * F), F32),
+            pltpu.VMEM((F, CH), F32),
             pltpu.VMEM((1, D), F32),
             pltpu.VMEM((T, 1, D), F32),
             pltpu.VMEM((1, D), F32),
             pltpu.VMEM((C, 1, D), F32),
             dma((3,)),
+            dma((micro, C)),
+            dma((micro, C)),
+            dma((micro, C)),
             dma((micro, C)),
             dma((micro, C)),
             dma((micro, C)),
@@ -393,7 +499,7 @@
             flops=flops, bytes_accessed=24 * D * F // 2, transcendentals=micro * TOK * F
         ),
         compiler_params=pltpu.CompilerParams(
-            collective_id=0, has_side_effects=True, vmem_limit_bytes=60 * 1024 * 1024
+            collective_id=0, has_side_effects=True, vmem_limit_bytes=52 * 1024 * 1024
         ),
     )(lengths, section_inputs[0], gain, cotangent, w_gate[0], w_up[0], w_down[0])
     gate, up, down, gain_out, rows = outs

time: 169 us -> 149 us (0.88)
  Pallas kernels: 161 us -> 144 us
  local copies, waits for them, and re-layouts: 6.75 us -> 4.48 us
    pallas_call x1, Pallas kernels: 161 us -> 144 us  [body(): pl.pallas_call(functools.partial(kernel, dims), out_shape=(pltpu.VMEM((CH...]
    unnamed x13 -> x5, local copies, waits for them, and re-layouts: 6.75 us -> 4.48 us
where the time goes in v2:
time: 149 us
  Pallas kernels  144 us (97%)
  local copies, waits for them, and re-layouts  4.48 us (3%)
    pallas_call x1, Pallas kernels, body(): pl.pallas_call(functools.partial(kernel, dims), out_shape=(pltpu.VMEM((CH...  144 us
    unnamed x5, local copies, waits for them, and re-layouts  4.48 us

profile of v2, /device:TPU:0, one launch (start us, length us, event | category | flops | bytes accessed | tf_op | source)
XLA Modules:
  0.0 148.7 jit_solution(1786188996974784660)
XLA Ops:
  0.6 143.5 %shard_map.110 = (bf16[1024,640]{1,0:T(8,128)(2,1)S(1)}, bf16[1024,640]{1,0:T(8,128)(2,1)S(1)}, bf16[640,1024]{1,0:T(8,128)(2,1)S(1)}, f32[1,4096]{1,0:T(1,128)S(1)}, bf16[2,16,4096]{2,1,0:T(8,128)(2,1)S(1)}) custom-call(s32[2,8]{1,0:T(2,128)} %len_ref.1, bf16[2,16,4096]{2,1,0:T(8,128)(2,1)} %bitcast.15, f32[1,4096]{1,0:T(1,128)} %gain_ref.1, ...), custom_call_target="tpu_custom_call" | custom-call | flops 10737418240 | bytes 31457280 | tf_op jit(solution)/shard_map/pallas_call | solution.py:446
  144.2 1.1 copy.17
  145.2 1.1 copy.18
  146.3 0.6 copy.20
  146.9 0.7 copy.21
  147.6 1.1 copy.19

commit v3 on v2

--- a/solution.py
+++ b/solution.py
@@ -38,9 +38,9 @@
     dims,
     len_ref, x_ref, gain_ref, cot_ref, wg_hbm, wu_hbm, wd_hbm,
     og_ref, ou_ref, od_ref, ogain_ref, orow_ref,
-    w2, wd, nbuf, ubuf, pbuf, rbuf, obuf, nstage, relay, nslice, uslice, gall, hall, act, ups, inv_buf,
+    w2, wd, nbuf, ubuf, pbuf, rbuf, obuf, nstage, relay, nslice, uslice, pall, hgrad, gall, hall, act, ups, inv_buf,
     accg, accd, gsum, gten, gdp_in, gdp,
-    s_w, s_n, r_n, s_u, r_u, s_p, r_p, s_o, r_hop, s_l, r_l, s_f, s_x, r_x, s_gain, r_gain, go,
+    s_w, s_n, r_n, s_u, r_u, s_p, r_p, s_o, r_hop, s_l, r_l, s_f, s_a, r_a, s_x, r_x, s_gain, r_gain, go,
 ):
     T, C, R, F, CH = dims
     D = C * CH
@@ -163,27 +163,51 @@
                 relay[m, c, t] = seeds(m, c)
 
     pl.semaphore_wait(barrier, (T - 1) + (C - 1) + T + middle + jnp.where(odd, 1, T))
+    def spread_n():
+        for m in range(MICRO):
+            for c in range(C):
+                spread(nbuf, m, c, s_n, r_n)
+
+    def slices_over_dp():
+        for m in range(MICRO):
+            for k in range(1, C):
+                j = dpeer(k)
+                send(nstage.at[m, j], nslice.at[m, d, t], s_a.at[m], r_a.at[m], {"dp": j})
+
+    def slices_over_tensor():
+        for m in range(MICRO):
+            wait_for(nslice.at[m, pl.ds(0, C - 1), 0], r_a.at[m])
+            for q in range(1, C):
+                owner = dpeer(q)
+                for k in range(1, T):
+                    send(nslice.at[m, owner, t], nslice.at[m, owner, t], s_x.at[m, 0], r_x.at[m, 0],
+                         {"tensor": tpeer(k)})
+
     @pl.when(s == 3)
     def _():
-        for c in range(C):
-            spread(nbuf, 0, c, s_n, r_n)
-        send_seeds(0)
+        for m in range(MICRO):
+            for c in range(C):
+                spread(nbuf, m, c, s_n, r_n)
+            send_seeds(m)
 
     @pl.when(s == 1)
     def _():
+        part = pl.ds(row, HALF)
+        slices_over_dp()
         for m in range(MICRO):
             for c in range(C):
                 spread_row(relay, m, c, s_l, r_l)
         for m in range(MICRO):
             for c in range(C):
                 wait_for(relay.at[m, c, pl.ds(0, HALF - 1)], r_l.at[m, c])
-                part = pl.ds(row, HALF)
                 send(relay.at[m, c, part], ubuf.at[m, c, part], s_f.at[m, c], r_u.at[m, c],
                      {"section": cross, "tensor": facing})
+        spread_n()
+        slices_over_tensor()
+        for m in range(MICRO):
             for c in range(C):
                 wait_for(relay.at[m, c, pl.ds(0, HALF)], s_f.at[m, c])
-            if m == 0:
-                pl.semaphore_signal(go, inc=1, device_id={"section": mate}, device_id_type=MESH)
+        pl.semaphore_signal(go, inc=1, device_id={"section": mate}, device_id_type=MESH)
 
     @pl.when(s == 2)
     def _():
@@ -195,20 +219,18 @@
 
     @pl.when(s == 0)
     def _():
+        slices_over_dp()
+        for c in range(C):
+            wait_for(relay.at[0, c], r_l.at[0, c])
+        spread_n()
+        slices_over_tensor()
         pl.semaphore_wait(go, 1)
         for m in range(MICRO):
             for c in range(C):
-                wait_for(relay.at[m, c], r_l.at[m, c])
+                if m > 0:
+                    wait_for(relay.at[m, c], r_l.at[m, c])
                 send(relay.at[m, c], nbuf.at[m, c], s_f.at[m, c], r_n.at[m, c],
                      {"section": cross, "tensor": facing})
-            for c in range(C):
-                wait_for(relay.at[m, c], s_f.at[m, c])
-
-    @pl.when(s < 2)
-    def _():
-        for m in range(MICRO):
-            for c in range(C):
-                spread(nbuf, m, c, s_n, r_n)
 
     for load in loads:
         load.wait()
@@ -229,42 +251,54 @@
     def forward(m):
         total = jnp.zeros((TOK, 2 * F), F32)
         for c in range(C):
+            @pl.when(s == 2)
+            def _():
+                wait_for(nbuf.at[m, c], r_n.at[m, c])
+
+            @pl.when(s != 2)
+            def _():
+                wait_for(others(nbuf, m, c), r_n.at[m, c])
             total += dot(rows_of(nbuf, m, c), w2[c * CH : (c + 1) * CH, :], NN)
-        pre_gate = total[:, :F]
+        pall[m, d] = total.astype(BF16)
+        exchange_all(pall, 2, m)
         pre_up = total[:, F:]
-        value, slope = gelu_parts(pre_gate)
+        value, slope = gelu_parts(total[:, :F])
         act[m] = value
         ups[m] = pre_up * slope
-        hall[m, d] = (value * pre_up).astype(BF16)
-        exchange_all(hall, 2, m)
-
-    def wait_n(m):
-        for c in range(C):
-            @pl.when(s == 2)
-            def _():
-                wait_for(nbuf.at[m, c], r_n.at[m, c])
-
-            @pl.when(s != 2)
-            def _():
-                wait_for(others(nbuf, m, c), r_n.at[m, c])
-
-    wait_n(0)
-    forward(0)
-    exchange_slices(nbuf, nslice, 0, 0)
-
-    @pl.when(s < 2)
-    def _():
-        wait_n(1)
-        exchange_slices(nbuf, nslice, 0, 1)
-        forward(1)
+
+        @pl.when(s >= 2)
+        def _():
+            exchange_slices(nbuf, nslice, 0, m)
+
+        @pl.when(s < 2)
+        def _():
+            nslice[m, d] = nbuf[m, d]
+
+    def expand(m):
+        wait_for(pall.at[m, pl.ds(0, C - 1)], r_x.at[m, 2])
+        wait_for(pall.at[m, pl.ds(0, C - 1)], s_x.at[m, 2])
+
+        def one(j, carry):
+            pre_gate = pall[m, j, :, :F].astype(F32)
+            pre_up = pall[m, j, :, F:].astype(F32)
+            value, slope = gelu_parts(pre_gate)
+            hall[m, j] = (value * pre_up).astype(BF16)
+            pall[m, j, :, :F] = (pre_up * slope).astype(BF16)
+            pall[m, j, :, F:] = value.astype(BF16)
+            return carry
+
+        lax.fori_loop(0, C, one, 0)
+
+    def expand_grads(m):
+        def one(j, carry):
+            upstream = hgrad[m, j].astype(F32)
+            gall[m, j, :, :F] = (upstream * pall[m, j, :, :F].astype(F32)).astype(BF16)
+            gall[m, j, :, F:] = (upstream * pall[m, j, :, F:].astype(F32)).astype(BF16)
+            return carry
+
+        lax.fori_loop(0, C, one, 0)
 
     def products(m):
-        @pl.when(s == 1)
-        def _():
-            for c in range(C):
-                wait_for(ubuf.at[m, c, t], r_hop.at[m, c])
-                spread(ubuf, m, c, s_u, r_u)
-
         grad_hidden = jnp.zeros((TOK, F), F32)
         for c in range(C):
             @pl.when(odd)
@@ -276,10 +310,11 @@
                 wait_for(ubuf.at[m, c], r_u.at[m, c])
             grad_hidden += dot(rows_of(ubuf, m, c), wd[:, c * CH : (c + 1) * CH], NT)
         exchange_slices(ubuf, uslice, 1, m)
-        gall[m, d, :, :F] = (grad_hidden * ups[m]).astype(BF16)
-        gall[m, d, :, F:] = (grad_hidden * act[m]).astype(BF16)
-        exchange_all(gall, 3, m)
-        both = gall[m, d]
+        hgrad[m, d] = grad_hidden.astype(BF16)
+        exchange_all(hgrad, 3, m)
+        both = jnp.concatenate(
+            [(grad_hidden * ups[m]).astype(BF16), (grad_hidden * act[m]).astype(BF16)], axis=1
+        )
         for c in range(C):
             term = dot(both, w2[c * CH : (c + 1) * CH, :], NT).astype(BF16)
             pbuf[m, c] = term.reshape(T, R, CH)
@@ -287,13 +322,6 @@
             for k in range(1, T):
                 j = tpeer(k)
                 send(pbuf.at[m, c, j], rbuf.at[m, c, t], s_p.at[m, c], r_p.at[m, c], {"tensor": j})
-        if m == 0:
-            @pl.when(s == 3)
-            def _():
-                for c in range(C):
-                    spread(nbuf, 1, c, s_n, r_n)
-                send_seeds(1)
-
     def finish(m):
         inv = inv_buf[m, :, 0:1]
         mean = jnp.zeros((R, 1), F32)
@@ -332,25 +360,42 @@
             def _():
                 send(obuf.at[m, c], ubuf.at[m, c, t], s_o.at[m, c], r_hop.at[m, c], {"section": s - 1})
 
+    forward(0)
+    pl.when(s < 2)(lambda: forward(1))
+
+    @pl.when(s == 1)
+    def _():
+        for m in range(MICRO):
+            for c in range(C):
+                wait_for(ubuf.at[m, c, t], r_hop.at[m, c])
+                spread(ubuf, m, c, s_u, r_u)
+
     products(0)
+    pl.when(s >= 2)(lambda: forward(1))
+    products(1)
+
+    @pl.when(s == 0)
+    def _():
+        for m in range(MICRO):
+            expand(m)
+
     finish(0)
-
-    @pl.when(s >= 2)
-    def _():
-        wait_n(1)
-        forward(1)
-        exchange_slices(nbuf, nslice, 0, 1)
-
-    products(1)
 
     count = C * TOK
     step = min(256, CH)
 
     def arrived(m):
-        wait_for(nslice.at[m, pl.ds(0, C - 1)], r_x.at[m, 0])
+        @pl.when(s >= 2)
+        def _():
+            wait_for(nslice.at[m, pl.ds(0, C - 1)], r_x.at[m, 0])
+
+        @pl.when(s < 2)
+        def _():
+            wait_for(nslice.at[m, pl.ds(0, C - 1), pl.ds(0, T - 1)], r_x.at[m, 0])
+
         wait_for(uslice.at[m, pl.ds(0, C - 1)], r_x.at[m, 1])
-        wait_for(hall.at[m, pl.ds(0, C - 1)], r_x.at[m, 2])
-        wait_for(gall.at[m, pl.ds(0, C - 1)], r_x.at[m, 3])
+        wait_for(hgrad.at[m, pl.ds(0, C - 1)], r_x.at[m, 3])
+        expand_grads(m)
 
     def term_gate_up(m, rows):
         return dot(nslice[m, :, :, :, rows].reshape(count, step), gall[m].reshape(count, 2 * F), TN)
@@ -372,7 +417,12 @@
     for k in range(1, T):
         send(gsum, gten.at[t], s_gain.at[0], r_gain.at[0], {"tensor": tpeer(k)})
 
-    pl.when(s > 0)(first_terms)
+    @pl.when(s > 0)
+    def _():
+        for m in range(MICRO):
+            expand(m)
+        first_terms()
+
     arrived(1)
     for n in range(CH // step):
         rows = slice(n * step, (n + 1) * step)
@@ -407,6 +457,10 @@
             def _():
                 wait_for(ubuf.at[m, c], s_o.at[m, c])
 
+            @pl.when(s == 0)
+            def _():
+                wait_for(relay.at[m, c], s_f.at[m, c])
+
             @pl.when(s == 1)
             def _():
                 wait_for(relay.at[m, c, pl.ds(0, HALF - 1)], s_l.at[m, c])
@@ -424,12 +478,29 @@
             def _():
                 wait_for(relay.at[m, c], s_l.at[m, c])
                 wait_for(obuf.at[m, c], s_o.at[m, c])
-        wait_for(nslice.at[m, pl.ds(0, C - 1)], s_x.at[m, 0])
+        @pl.when(s >= 2)
+        def _():
+            wait_for(nslice.at[m, pl.ds(0, C - 1)], s_x.at[m, 0])
+
+        @pl.when(s < 2)
+        def _():
+            wait_for(nslice.at[m, pl.ds(0, C - 1), 0], s_a.at[m])
+            wait_for(nslice.at[m, pl.ds(0, C - 1), pl.ds(0, T - 1)], s_x.at[m, 0])
+
         wait_for(uslice.at[m, pl.ds(0, C - 1)], s_x.at[m, 1])
-        wait_for(hall.at[m, pl.ds(0, C - 1)], s_x.at[m, 2])
-        wait_for(gall.at[m, pl.ds(0, C - 1)], s_x.at[m, 3])
+        wait_for(hgrad.at[m, pl.ds(0, C - 1)], s_x.at[m, 3])
     wait_for(gten.at[pl.ds(0, T - 1)], s_gain.at[0])
     wait_for(gdp.at[pl.ds(0, C - 1)], s_gain.at[1])
+
+
+def writer(*refs):
+    count = len(refs) // 2
+    sems = refs[-1]
+    copies = [pltpu.make_async_copy(refs[i], refs[count + i], sems.at[i]) for i in range(count)]
+    for copy in copies:
+        copy.start()
+    for copy in copies:
+        copy.wait()
 
 
 def body(T, C, section_inputs, gain, w_gate, w_up, w_down, cotangent, lengths):
@@ -468,6 +539,8 @@
             pltpu.VMEM((micro, C, T, R, CH), BF16),
             pltpu.VMEM((micro, C, TOK, 2 * F), BF16),
             pltpu.VMEM((micro, C, TOK, F), BF16),
+            pltpu.VMEM((micro, C, TOK, 2 * F), BF16),
+            pltpu.VMEM((micro, C, TOK, F), BF16),
             pltpu.VMEM((micro, TOK, F), F32),
             pltpu.VMEM((micro, TOK, F), F32),
             pltpu.VMEM((micro, R, 128), F32),
@@ -489,6 +562,8 @@
             dma((micro, C)),
             dma((micro, C)),
             dma((micro, C)),
+            dma((micro,)),
+            dma((micro,)),
             dma((micro, 4)),
             dma((micro, 4)),
             dma((2,)),
@@ -499,10 +574,16 @@
             flops=flops, bytes_accessed=24 * D * F // 2, transcendentals=micro * TOK * F
         ),
         compiler_params=pltpu.CompilerParams(
-            collective_id=0, has_side_effects=True, vmem_limit_bytes=52 * 1024 * 1024
+            collective_id=0, has_side_effects=True, vmem_limit_bytes=54 * 1024 * 1024
         ),
     )(lengths, section_inputs[0], gain, cotangent, w_gate[0], w_up[0], w_down[0])
-    gate, up, down, gain_out, rows = outs
+    gate, up, down, gain_out, rows = pl.pallas_call(
+        writer,
+        out_shape=tuple(jax.ShapeDtypeStruct(out.shape, out.dtype) for out in outs),
+        in_specs=[vmem] * len(outs),
+        out_specs=(hbm,) * len(outs),
+        scratch_shapes=[dma((len(outs),))],
+    )(*outs)
     return (gate[None], up[None], down[None], gain_out, rows[None])
 
 

time: 149 us -> 141 us (0.946)
  Pallas kernels: 144 us -> 136 us
    pallas_call x1, Pallas kernels: 144 us -> 131 us  [body(): pl.pallas_call(functools.partial(kernel, dims), out_shape=(pltpu.VMEM((CH...]
    pallas_call x0 -> x1, Pallas kernels: none -> 4.19 us  [body(): pl.pallas_call(writer, out_shape=tuple((jax.ShapeDtypeStruct(out.shape, o...]
    unnamed x5 -> x10, local copies, waits for them, and re-layouts: 4.48 us -> 4.49 us
where the time goes in v3:
time: 141 us
  Pallas kernels  136 us (96%)
  local copies, waits for them, and re-layouts  4.49 us (3%)
    pallas_call x1, Pallas kernels, body(): pl.pallas_call(functools.partial(kernel, dims), out_shape=(pltpu.VMEM((CH...  131 us
    unnamed x10, local copies, waits for them, and re-layouts  4.49 us
    pallas_call x1, Pallas kernels, body(): pl.pallas_call(writer, out_shape=tuple((jax.ShapeDtypeStruct(out.shape, o...  4.19 us

profile of v3, /device:TPU:0, one launch (start us, length us, event | category | flops | bytes accessed | tf_op | source)
XLA Modules:
  0.0 140.9 jit_solution(3080785346436373456)
XLA Ops:
  0.6 131.4 %shard_map.110 = (bf16[1024,640]{1,0:T(8,128)(2,1)S(1)}, bf16[1024,640]{1,0:T(8,128)(2,1)S(1)}, bf16[640,1024]{1,0:T(8,128)(2,1)S(1)}, f32[1,4096]{1,0:T(1,128)S(1)}, bf16[2,16,4096]{2,1,0:T(8,128)(2,1)S(1)}) custom-call(s32[2,8]{1,0:T(2,128)} %len_ref.1, bf16[2,16,4096]{2,1,0:T(8,128)(2,1)} %bitcast.14, f32[1,4096]{1,0:T(1,128)} %gain_ref.1, ...), custom_call_target="tpu_custom_call" | custom-call | flops 10737418240 | bytes 31457280 | tf_op jit(solution)/shard_map/pallas_call | solution.py:517
  132.0 0.0 copy-start
  132.1 1.1 copy-done
  133.1 0.0 copy-start.1
  133.1 1.1 copy-done.1
  134.2 0.0 copy-start.2
  134.2 1.1 copy-done.2
  135.3 0.0 copy-start.3
  135.3 0.7 copy-done.3
  135.9 0.0 copy-start.4
  135.9 0.6 copy-done.4
  136.5 4.2 %shard_map.111 = (bf16[1024,640]{1,0:T(8,128)(2,1)}, bf16[1024,640]{1,0:T(8,128)(2,1)}, bf16[640,1024]{1,0:T(8,128)(2,1)}, f32[1,4096]{1,0:T(1,128)}, bf16[2,16,4096]{2,1,0:T(8,128)(2,1)}) custom-call(bf16[1024,640]{1,0:T(8,128)(2,1)} %copy-done, bf16[1024,640]{1,0:T(8,128)(2,1)} %copy-done.1, bf16[640,1024]{1,0:T(8,128)(2,1)} %copy-done.2, ...), custom_call_target="tpu_custom_call" | custom-call | tf_op jit(solution)/shard_map/pallas_call | solution.py:580
Async XLA Ops:
  132.0 1.1 copy-start
  133.1 1.1 copy-start.1
  134.2 1.1 copy-start.2
  135.3 0.7 copy-start.3
  135.9 0.6 copy-start.4

commit v4 on v3

--- a/solution.py
+++ b/solution.py
@@ -36,11 +36,11 @@
 
 def kernel(
     dims,
-    len_ref, x_ref, gain_ref, cot_ref, wg_hbm, wu_hbm, wd_hbm,
-    og_ref, ou_ref, od_ref, ogain_ref, orow_ref,
-    w2, wd, nbuf, ubuf, pbuf, rbuf, obuf, nstage, relay, nslice, uslice, pall, hgrad, gall, hall, act, ups, inv_buf,
-    accg, accd, gsum, gten, gdp_in, gdp,
-    s_w, s_n, r_n, s_u, r_u, s_p, r_p, s_o, r_hop, s_l, r_l, s_f, s_a, r_a, s_x, r_x, s_gain, r_gain, go,
+    len_ref, x_hbm, gain_hbm, cot_hbm, wg_hbm, wu_hbm, wd_hbm,
+    od_ref, ogain_ref, orow_ref, accg, nslice, gall,
+    x_ref, gain_ref, cot_ref, w2, wd, wdt, nbuf, ubuf, pbuf, rbuf, obuf, nstage, relay, uslice, pall, hgrad, hall, act, ups, inv_buf,
+    accd, gsum, gten, gdp_in, gdp,
+    s_w, s_d, s_n, r_n, s_u, r_u, s_p, r_p, s_o, r_hop, s_l, r_l, s_f, s_a, r_a, s_x, r_x, s_gain, r_gain, go,
 ):
     T, C, R, F, CH = dims
     D = C * CH
@@ -50,14 +50,6 @@
     t = lax.axis_index("tensor")
     d = lax.axis_index("dp")
 
-    loads = [
-        pltpu.make_async_copy(wg_hbm, w2.at[:, pl.ds(0, F)], s_w.at[0]),
-        pltpu.make_async_copy(wu_hbm, w2.at[:, pl.ds(F, F)], s_w.at[1]),
-        pltpu.make_async_copy(wd_hbm, wd, s_w.at[2]),
-    ]
-    for load in loads:
-        load.start()
-
     def tpeer(k):
         return lax.rem(t + k, T)
 
@@ -116,6 +108,25 @@
     def others(buf, m, c):
         return buf.at[m, c, pl.ds(0, T - 1)]
 
+    inputs = [
+        pltpu.make_async_copy(x_hbm, x_ref, s_w.at[3]),
+        pltpu.make_async_copy(gain_hbm, gain_ref, s_w.at[4]),
+        pltpu.make_async_copy(cot_hbm, cot_ref, s_w.at[5]),
+    ]
+    for load in inputs:
+        load.start()
+    loads = [
+        pltpu.make_async_copy(wg_hbm, w2.at[:, pl.ds(0, F)], s_w.at[0]),
+        pltpu.make_async_copy(wu_hbm, w2.at[:, pl.ds(F, F)], s_w.at[1]),
+    ]
+    for load in loads:
+        load.start()
+    for c in range(min(2, C)):
+        pltpu.make_async_copy(wd_hbm.at[:, pl.ds(c * CH, CH)], wd.at[c], s_d.at[c]).start()
+
+    for load in inputs:
+        load.wait()
+
     keep_pos = lax.broadcasted_iota(jnp.int32, (R, 1), 0)
     for m in range(MICRO):
         square = jnp.zeros((R, 1), F32)
@@ -185,10 +196,9 @@
 
     @pl.when(s == 3)
     def _():
-        for m in range(MICRO):
-            for c in range(C):
-                spread(nbuf, m, c, s_n, r_n)
-            send_seeds(m)
+        for c in range(C):
+            spread(nbuf, 0, c, s_n, r_n)
+        send_seeds(0)
 
     @pl.when(s == 1)
     def _():
@@ -232,6 +242,17 @@
                 send(relay.at[m, c], nbuf.at[m, c], s_f.at[m, c], r_n.at[m, c],
                      {"section": cross, "tensor": facing})
 
+    def down_load(c):
+        slot = c % 2
+        return pltpu.make_async_copy(wd_hbm.at[:, pl.ds(c * CH, CH)], wd.at[slot], s_d.at[slot])
+
+    for c in range(C):
+        down_load(c).wait()
+        half = max(128, CH // 2)
+        for n in range(CH // half):
+            wdt[c * CH + n * half : c * CH + (n + 1) * half, :] = wd[c % 2, :, n * half : (n + 1) * half].T
+        if c + 2 < C:
+            down_load(c + 2).start()
     for load in loads:
         load.wait()
 
@@ -258,6 +279,10 @@
             @pl.when(s != 2)
             def _():
                 wait_for(others(nbuf, m, c), r_n.at[m, c])
+            if m == 0:
+                @pl.when(s == 3)
+                def _():
+                    spread(nbuf, 1, c, s_n, r_n)
             total += dot(rows_of(nbuf, m, c), w2[c * CH : (c + 1) * CH, :], NN)
         pall[m, d] = total.astype(BF16)
         exchange_all(pall, 2, m)
@@ -291,9 +316,9 @@
 
     def expand_grads(m):
         def one(j, carry):
-            upstream = hgrad[m, j].astype(F32)
-            gall[m, j, :, :F] = (upstream * pall[m, j, :, :F].astype(F32)).astype(BF16)
-            gall[m, j, :, F:] = (upstream * pall[m, j, :, F:].astype(F32)).astype(BF16)
+            upstream = hgrad[m, j]
+            gall[m, j, :, :F] = upstream * pall[m, j, :, :F]
+            gall[m, j, :, F:] = upstream * pall[m, j, :, F:]
             return carry
 
         lax.fori_loop(0, C, one, 0)
@@ -308,7 +333,11 @@
             @pl.when(jnp.logical_not(odd))
             def _():
                 wait_for(ubuf.at[m, c], r_u.at[m, c])
-            grad_hidden += dot(rows_of(ubuf, m, c), wd[:, c * CH : (c + 1) * CH], NT)
+            if m == 0:
+                @pl.when(s == 3)
+                def _():
+                    spread_row(ubuf, 1, c, s_u, r_u)
+            grad_hidden += dot(rows_of(ubuf, m, c), wdt[c * CH : (c + 1) * CH, :], NN)
         exchange_slices(ubuf, uslice, 1, m)
         hgrad[m, d] = grad_hidden.astype(BF16)
         exchange_all(hgrad, 3, m)
@@ -370,21 +399,21 @@
                 wait_for(ubuf.at[m, c, t], r_hop.at[m, c])
                 spread(ubuf, m, c, s_u, r_u)
 
+    @pl.when(s == 0)
+    def _():
+        for m in range(MICRO):
+            expand(m)
+
     products(0)
     pl.when(s >= 2)(lambda: forward(1))
     products(1)
 
-    @pl.when(s == 0)
-    def _():
-        for m in range(MICRO):
-            expand(m)
-
     finish(0)
 
     count = C * TOK
     step = min(256, CH)
 
-    def arrived(m):
+    def slices_arrived(m):
         @pl.when(s >= 2)
         def _():
             wait_for(nslice.at[m, pl.ds(0, C - 1)], r_x.at[m, 0])
@@ -394,21 +423,23 @@
             wait_for(nslice.at[m, pl.ds(0, C - 1), pl.ds(0, T - 1)], r_x.at[m, 0])
 
         wait_for(uslice.at[m, pl.ds(0, C - 1)], r_x.at[m, 1])
+
+    def grads_arrived(m):
         wait_for(hgrad.at[m, pl.ds(0, C - 1)], r_x.at[m, 3])
         expand_grads(m)
 
-    def term_gate_up(m, rows):
-        return dot(nslice[m, :, :, :, rows].reshape(count, step), gall[m].reshape(count, 2 * F), TN)
-
     def term_down(m, cols):
         return dot(hall[m].reshape(count, F), uslice[m, :, :, :, cols].reshape(count, step), TN)
 
     def first_terms():
-        arrived(0)
+        slices_arrived(0)
+        for n in range(CH // step):
+            cols = slice(n * step, (n + 1) * step)
+            accd[:, cols] = term_down(0, cols)
+        grads_arrived(0)
         for n in range(CH // step):
             part = slice(n * step, (n + 1) * step)
-            accg[part, :] = term_gate_up(0, part)
-            accd[:, part] = term_down(0, part)
+            accg[part, :] = gate_up_term(nslice, gall, 0, part)
 
     pl.when(s == 0)(first_terms)
     finish(1)
@@ -421,14 +452,12 @@
     def _():
         for m in range(MICRO):
             expand(m)
-        first_terms()
-
-    arrived(1)
+
+    pl.when(s > 0)(first_terms)
+    slices_arrived(1)
     for n in range(CH // step):
-        rows = slice(n * step, (n + 1) * step)
-        total = accg[rows, :] + term_gate_up(1, rows)
-        og_ref[rows, :] = total[:, :F].astype(BF16)
-        ou_ref[rows, :] = total[:, F:].astype(BF16)
+        cols = slice(n * step, (n + 1) * step)
+        od_ref[:, cols] = (accd[:, cols] + term_down(1, cols)).astype(BF16)
 
     wait_for(gten.at[pl.ds(0, T - 1)], r_gain.at[0])
     gain_total = gten[0]
@@ -439,9 +468,7 @@
     for k in range(1, C):
         send(gdp_in, gdp.at[d], s_gain.at[1], r_gain.at[1], {"dp": dpeer(k)})
 
-    for n in range(CH // step):
-        cols = slice(n * step, (n + 1) * step)
-        od_ref[:, cols] = (accd[:, cols] + term_down(1, cols)).astype(BF16)
+    grads_arrived(1)
 
     wait_for(gdp.at[pl.ds(0, C - 1)], r_gain.at[1])
     gain_total = gdp[0]
@@ -493,12 +520,33 @@
     wait_for(gdp.at[pl.ds(0, C - 1)], s_gain.at[1])
 
 
-def writer(*refs):
-    count = len(refs) // 2
-    sems = refs[-1]
-    copies = [pltpu.make_async_copy(refs[i], refs[count + i], sems.at[i]) for i in range(count)]
+def gate_up_term(nslice, gall, m, rows):
+    C, T, R, _ = nslice.shape[1:]
+    step = rows.stop - rows.start
+    left = nslice[m, :, :, :, rows].reshape(C * T * R, step)
+    return dot(left, gall[m].reshape(C * T * R, gall.shape[-1]), TN)
+
+
+def writer(down, gain, rows, accg, nslice, gall, og, ou, od, ogain, orow, vg, vu, sems, tile_sems):
+    copies = [
+        pltpu.make_async_copy(down, od, sems.at[0]),
+        pltpu.make_async_copy(gain, ogain, sems.at[1]),
+        pltpu.make_async_copy(rows, orow, sems.at[2]),
+    ]
     for copy in copies:
         copy.start()
+    CH, F = vg.shape
+    step = min(256, CH)
+    for n in range(CH // step):
+        part = slice(n * step, (n + 1) * step)
+        total = accg[part, :] + gate_up_term(nslice, gall, MICRO - 1, part)
+        vg[part, :] = total[:, :F].astype(BF16)
+        vu[part, :] = total[:, F:].astype(BF16)
+        for which, (src, dst) in enumerate(((vg, og), (vu, ou))):
+            block = pl.ds(n * step, step)
+            copy = pltpu.make_async_copy(src.at[block], dst.at[block], tile_sems.at[which, n])
+            copy.start()
+            copies.append(copy)
     for copy in copies:
         copy.wait()
 
@@ -517,17 +565,22 @@
     outs = pl.pallas_call(
         functools.partial(kernel, dims),
         out_shape=(
-            pltpu.VMEM((CH, F), BF16),
-            pltpu.VMEM((CH, F), BF16),
             pltpu.VMEM((F, CH), BF16),
             pltpu.VMEM((1, D), F32),
             pltpu.VMEM((micro, R, D), BF16),
+            pltpu.VMEM((CH, 2 * F), F32),
+            pltpu.VMEM((micro, C, T, R, CH), BF16),
+            pltpu.VMEM((micro, C, TOK, 2 * F), BF16),
         ),
-        in_specs=[smem, vmem, vmem, vmem, hbm, hbm, hbm],
-        out_specs=(vmem, vmem, vmem, vmem, vmem),
+        in_specs=[smem] + [hbm] * 6,
+        out_specs=(vmem,) * 6,
         scratch_shapes=[
+            pltpu.VMEM((micro, R, D), BF16),
+            pltpu.VMEM((1, D), F32),
+            pltpu.VMEM((micro, R, D), BF16),
             pltpu.VMEM((D, 2 * F), BF16),
-            pltpu.VMEM((F, D), BF16),
+            pltpu.VMEM((2, F, CH), BF16),
+            pltpu.VMEM((D, F), BF16),
             pltpu.VMEM((micro, C, T, R, CH), BF16),
             pltpu.VMEM((micro, C, T, R, CH), BF16),
             pltpu.VMEM((micro, C, T, R, CH), BF16),
@@ -536,21 +589,19 @@
             pltpu.VMEM((micro, C, R, CH), BF16),
             pltpu.VMEM((micro, C, T, R, CH), BF16),
             pltpu.VMEM((micro, C, T, R, CH), BF16),
-            pltpu.VMEM((micro, C, T, R, CH), BF16),
             pltpu.VMEM((micro, C, TOK, 2 * F), BF16),
             pltpu.VMEM((micro, C, TOK, F), BF16),
-            pltpu.VMEM((micro, C, TOK, 2 * F), BF16),
             pltpu.VMEM((micro, C, TOK, F), BF16),
             pltpu.VMEM((micro, TOK, F), F32),
             pltpu.VMEM((micro, TOK, F), F32),
             pltpu.VMEM((micro, R, 128), F32),
-            pltpu.VMEM((CH, 2 * F), F32),
             pltpu.VMEM((F, CH), F32),
             pltpu.VMEM((1, D), F32),
             pltpu.VMEM((T, 1, D), F32),
             pltpu.VMEM((1, D), F32),
             pltpu.VMEM((C, 1, D), F32),
-            dma((3,)),
+            dma((6,)),
+            dma((2,)),
             dma((micro, C)),
             dma((micro, C)),
             dma((micro, C)),
@@ -574,15 +625,27 @@
             flops=flops, bytes_accessed=24 * D * F // 2, transcendentals=micro * TOK * F
         ),
         compiler_params=pltpu.CompilerParams(
-            collective_id=0, has_side_effects=True, vmem_limit_bytes=54 * 1024 * 1024
+            collective_id=0, has_side_effects=True, vmem_limit_bytes=46 * 1024 * 1024
         ),
     )(lengths, section_inputs[0], gain, cotangent, w_gate[0], w_up[0], w_down[0])
     gate, up, down, gain_out, rows = pl.pallas_call(
         writer,
-        out_shape=tuple(jax.ShapeDtypeStruct(out.shape, out.dtype) for out in outs),
+        out_shape=(
+            jax.ShapeDtypeStruct((CH, F), BF16),
+            jax.ShapeDtypeStruct((CH, F), BF16),
+            jax.ShapeDtypeStruct((F, CH), BF16),
+            jax.ShapeDtypeStruct((1, D), F32),
+            jax.ShapeDtypeStruct((micro, R, D), BF16),
+        ),
         in_specs=[vmem] * len(outs),
-        out_specs=(hbm,) * len(outs),
-        scratch_shapes=[dma((len(outs),))],
+        out_specs=(hbm,) * 5,
+        scratch_shapes=[
+            pltpu.VMEM((CH, F), BF16),
+            pltpu.VMEM((CH, F), BF16),
+            dma((3,)),
+            dma((2, max(1, CH // 256))),
+        ],
+        compiler_params=pltpu.CompilerParams(vmem_limit_bytes=14 * 1024 * 1024),
     )(*outs)
     return (gate[None], up[None], down[None], gain_out, rows[None])
 

time: 141 us -> 130 us (0.922)
  Pallas kernels: 136 us -> 129 us
  local copies, waits for them, and re-layouts: 4.49 us -> 0 us
    pallas_call x2, Pallas kernels: 136 us -> 129 us  [the longest x1 127 us: body(): pl.pallas_call(functools.partial(kernel, dims), out_shape=(pltpu.VMEM((F,...]
    unnamed x10 -> x0, local copies, waits for them, and re-layouts: 4.49 us -> none
where the time goes in v4:
time: 130 us
  Pallas kernels  129 us (99%)
    pallas_call x1, Pallas kernels, body(): pl.pallas_call(functools.partial(kernel, dims), out_shape=(pltpu.VMEM((F,...  127 us

profile of v4, /device:TPU:0, one launch (start us, length us, event | category | flops | bytes accessed | tf_op | source)
XLA Modules:
  0.0 130.3 jit_solution(6655135235890731119)
XLA Ops:
  0.6 127.1 %shard_map.110 = (bf16[640,1024]{1,0:T(8,128)(2,1)S(1)}, f32[1,4096]{1,0:T(1,128)S(1)}, bf16[2,16,4096]{2,1,0:T(8,128)(2,1)S(1)}, f32[1024,1280]{1,0:T(8,128)S(1...) custom-call(s32[2,8]{1,0:T(2,128)} %len_ref.1, bf16[2,16,4096]{2,1,0:T(8,128)(2,1)} %bitcast.14, ...), custom_call_target="tpu_custom_call" | custom-call | flops 10737418240 | bytes 31457280 | tf_op jit(solution)/shard_map/pallas_call | solution.py:565
  127.7 2.4 %shard_map.111 = (bf16[1024,640]{1,0:T(8,128)(2,1)}, bf16[1024,640]{1,0:T(8,128)(2,1)}, bf16[640,1024]{1,0:T(8,128)(2,1)}, f32[1,4096]{1,0:T(1,128)}, bf16[2,16,4096]{2,1,0:T(8,128)(2,1)}) custom-call(bf16[640,1024]{1,0:T(8,128)(2,1)S(1)} %get-tuple-element.16.down, f32[1,4096]{1,0:T(1,128)S(1)} %get-tuple-element.17.gain, ...), custom_call_target="tpu_custom_call" | custom-call | tf_op jit(solution)/shard_map/pallas_call | solution.py:631

commit v5 on v4

--- a/solution.py
+++ b/solution.py
@@ -37,8 +37,8 @@
 def kernel(
     dims,
     len_ref, x_hbm, gain_hbm, cot_hbm, wg_hbm, wu_hbm, wd_hbm,
-    od_ref, ogain_ref, orow_ref, accg, nslice, gall,
-    x_ref, gain_ref, cot_ref, w2, wd, wdt, nbuf, ubuf, pbuf, rbuf, obuf, nstage, relay, uslice, pall, hgrad, hall, act, ups, inv_buf,
+    od_ref, ogain_ref, orow_ref, accg, nslice, pall,
+    x_ref, gain_ref, cot_ref, w2, w2t, wd, wdt, nbuf, ubuf, pbuf, rbuf, obuf, nstage, relay, uslice, hgrad, hall, act, ups, inv_buf,
     accd, gsum, gten, gdp_in, gdp,
     s_w, s_d, s_n, r_n, s_u, r_u, s_p, r_p, s_o, r_hop, s_l, r_l, s_f, s_a, r_a, s_x, r_x, s_gain, r_gain, go,
 ):
@@ -50,8 +50,14 @@
     t = lax.axis_index("tensor")
     d = lax.axis_index("dp")
 
+    rings = sorted(range(HALF), key=lambda q: -min(q, HALF - q))
+    offsets = [(dy, dz) for dz in rings for dy in (1, 0)]
+    line = t // HALF
+    place = lax.rem(t, HALF)
+
     def tpeer(k):
-        return lax.rem(t + k, T)
+        dy, dz = offsets[k - 1]
+        return (1 - line if dy else line) * HALF + lax.rem(place + dz, HALF)
 
     def dpeer(k):
         return lax.rem(d + k, C)
@@ -121,8 +127,9 @@
     ]
     for load in loads:
         load.start()
-    for c in range(min(2, C)):
-        pltpu.make_async_copy(wd_hbm.at[:, pl.ds(c * CH, CH)], wd.at[c], s_d.at[c]).start()
+    lead = max(128, CH // 4)
+    for n in range(2):
+        pltpu.make_async_copy(wd_hbm.at[:, pl.ds(n * lead, lead)], wd.at[n], s_d.at[n]).start()
 
     for load in inputs:
         load.wait()
@@ -242,17 +249,17 @@
                 send(relay.at[m, c], nbuf.at[m, c], s_f.at[m, c], r_n.at[m, c],
                      {"section": cross, "tensor": facing})
 
-    def down_load(c):
-        slot = c % 2
-        return pltpu.make_async_copy(wd_hbm.at[:, pl.ds(c * CH, CH)], wd.at[slot], s_d.at[slot])
-
-    for c in range(C):
-        down_load(c).wait()
-        half = max(128, CH // 2)
-        for n in range(CH // half):
-            wdt[c * CH + n * half : c * CH + (n + 1) * half, :] = wd[c % 2, :, n * half : (n + 1) * half].T
-        if c + 2 < C:
-            down_load(c + 2).start()
+    half = max(128, CH // 4)
+    pieces = D // half
+
+    def down_load(n):
+        return pltpu.make_async_copy(wd_hbm.at[:, pl.ds(n * half, half)], wd.at[n % 2], s_d.at[n % 2])
+
+    for n in range(pieces):
+        down_load(n).wait()
+        wdt[n * half : (n + 1) * half, :] = wd[n % 2].T
+        if n + 2 < pieces:
+            down_load(n + 2).start()
     for load in loads:
         load.wait()
 
@@ -284,6 +291,10 @@
                 def _():
                     spread(nbuf, 1, c, s_n, r_n)
             total += dot(rows_of(nbuf, m, c), w2[c * CH : (c + 1) * CH, :], NN)
+            if m == 0:
+                for n in range(CH // half):
+                    part = slice(c * CH + n * half, c * CH + (n + 1) * half)
+                    w2t[:, part] = w2[part, :].T
         pall[m, d] = total.astype(BF16)
         exchange_all(pall, 2, m)
         pre_up = total[:, F:]
@@ -317,8 +328,8 @@
     def expand_grads(m):
         def one(j, carry):
             upstream = hgrad[m, j]
-            gall[m, j, :, :F] = upstream * pall[m, j, :, :F]
-            gall[m, j, :, F:] = upstream * pall[m, j, :, F:]
+            pall[m, j, :, :F] = upstream * pall[m, j, :, :F]
+            pall[m, j, :, F:] = upstream * pall[m, j, :, F:]
             return carry
 
         lax.fori_loop(0, C, one, 0)
@@ -345,12 +356,16 @@
             [(grad_hidden * ups[m]).astype(BF16), (grad_hidden * act[m]).astype(BF16)], axis=1
         )
         for c in range(C):
-            term = dot(both, w2[c * CH : (c + 1) * CH, :], NT).astype(BF16)
+            term = dot(both, w2t[:, c * CH : (c + 1) * CH], NN).astype(BF16)
             pbuf[m, c] = term.reshape(T, R, CH)
             rbuf[m, c, t] = pbuf[m, c, t]
             for k in range(1, T):
                 j = tpeer(k)
                 send(pbuf.at[m, c, j], rbuf.at[m, c, t], s_p.at[m, c], r_p.at[m, c], {"tensor": j})
+    def send_gain():
+        for k in range(1, T):
+            send(gsum, gten.at[t], s_gain.at[0], r_gain.at[0], {"tensor": tpeer(k)})
+
     def finish(m):
         inv = inv_buf[m, :, 0:1]
         mean = jnp.zeros((R, 1), F32)
@@ -370,6 +385,8 @@
             else:
                 gsum[:, cols] += gain_part
             sums.append(scaled)
+        if m == MICRO - 1:
+            pl.when(s == 0)(send_gain)
         factor = inv * inv * inv * (mean * (1.0 / D))
         for c in range(C):
             cols = slice(c * CH, (c + 1) * CH)
@@ -381,9 +398,9 @@
 
             @pl.when(odd)
             def _():
-                for k in range(T):
+                for k in range(1, T + 1):
                     send(obuf.at[m, c], ubuf.at[m, c, t], s_o.at[m, c], r_u.at[m, c],
-                         {"section": s - 1, "tensor": lax.rem(t + k, T)})
+                         {"section": s - 1, "tensor": tpeer(k)})
 
             @pl.when(s == 2)
             def _():
@@ -439,14 +456,13 @@
         grads_arrived(0)
         for n in range(CH // step):
             part = slice(n * step, (n + 1) * step)
-            accg[part, :] = gate_up_term(nslice, gall, 0, part)
+            accg[part, :] = gate_up_term(nslice, pall, 0, part)
 
     pl.when(s == 0)(first_terms)
     finish(1)
 
     gten[t] = gsum[...]
-    for k in range(1, T):
-        send(gsum, gten.at[t], s_gain.at[0], r_gain.at[0], {"tensor": tpeer(k)})
+    pl.when(s > 0)(send_gain)
 
     @pl.when(s > 0)
     def _():
@@ -470,52 +486,51 @@
 
     grads_arrived(1)
 
+    for m in range(MICRO):
+        for c in range(C):
+            wait_for(others(pbuf, m, c), s_p.at[m, c])
+
+            @pl.when(odd)
+            def _():
+                wait_for(ubuf.at[m, c], s_o.at[m, c])
+
+            @pl.when(s == 0)
+            def _():
+                wait_for(relay.at[m, c], s_f.at[m, c])
+
+            @pl.when(s == 1)
+            def _():
+                wait_for(relay.at[m, c, pl.ds(0, HALF - 1)], s_l.at[m, c])
+                wait_for(others(ubuf, m, c), s_u.at[m, c])
+
+            @pl.when(s == 3)
+            def _():
+                wait_for(ubuf.at[m, c, pl.ds(0, HALF - 1)], s_u.at[m, c])
+
+            @pl.when(s != 2)
+            def _():
+                wait_for(others(nbuf, m, c), s_n.at[m, c])
+
+            @pl.when(s == 2)
+            def _():
+                wait_for(relay.at[m, c], s_l.at[m, c])
+                wait_for(obuf.at[m, c], s_o.at[m, c])
+        @pl.when(s >= 2)
+        def _():
+            wait_for(nslice.at[m, pl.ds(0, C - 1)], s_x.at[m, 0])
+
+        @pl.when(s < 2)
+        def _():
+            wait_for(nslice.at[m, pl.ds(0, C - 1), 0], s_a.at[m])
+            wait_for(nslice.at[m, pl.ds(0, C - 1), pl.ds(0, T - 1)], s_x.at[m, 0])
+
+        wait_for(uslice.at[m, pl.ds(0, C - 1)], s_x.at[m, 1])
+        wait_for(hgrad.at[m, pl.ds(0, C - 1)], s_x.at[m, 3])
     wait_for(gdp.at[pl.ds(0, C - 1)], r_gain.at[1])
     gain_total = gdp[0]
     for j in range(1, C):
         gain_total += gdp[j]
     ogain_ref[...] = gain_total
-
-    for m in range(MICRO):
-        for c in range(C):
-            wait_for(others(pbuf, m, c), s_p.at[m, c])
-
-            @pl.when(odd)
-            def _():
-                wait_for(ubuf.at[m, c], s_o.at[m, c])
-
-            @pl.when(s == 0)
-            def _():
-                wait_for(relay.at[m, c], s_f.at[m, c])
-
-            @pl.when(s == 1)
-            def _():
-                wait_for(relay.at[m, c, pl.ds(0, HALF - 1)], s_l.at[m, c])
-                wait_for(others(ubuf, m, c), s_u.at[m, c])
-
-            @pl.when(s == 3)
-            def _():
-                wait_for(ubuf.at[m, c, pl.ds(0, HALF - 1)], s_u.at[m, c])
-
-            @pl.when(s != 2)
-            def _():
-                wait_for(others(nbuf, m, c), s_n.at[m, c])
-
-            @pl.when(s == 2)
-            def _():
-                wait_for(relay.at[m, c], s_l.at[m, c])
-                wait_for(obuf.at[m, c], s_o.at[m, c])
-        @pl.when(s >= 2)
-        def _():
-            wait_for(nslice.at[m, pl.ds(0, C - 1)], s_x.at[m, 0])
-
-        @pl.when(s < 2)
-        def _():
-            wait_for(nslice.at[m, pl.ds(0, C - 1), 0], s_a.at[m])
-            wait_for(nslice.at[m, pl.ds(0, C - 1), pl.ds(0, T - 1)], s_x.at[m, 0])
-
-        wait_for(uslice.at[m, pl.ds(0, C - 1)], s_x.at[m, 1])
-        wait_for(hgrad.at[m, pl.ds(0, C - 1)], s_x.at[m, 3])
     wait_for(gten.at[pl.ds(0, T - 1)], s_gain.at[0])
     wait_for(gdp.at[pl.ds(0, C - 1)], s_gain.at[1])
 
@@ -579,7 +594,8 @@
             pltpu.VMEM((1, D), F32),
             pltpu.VMEM((micro, R, D), BF16),
             pltpu.VMEM((D, 2 * F), BF16),
-            pltpu.VMEM((2, F, CH), BF16),
+            pltpu.VMEM((2 * F, D), BF16),
+            pltpu.VMEM((2, F, max(128, CH // 4)), BF16),
             pltpu.VMEM((D, F), BF16),
             pltpu.VMEM((micro, C, T, R, CH), BF16),
             pltpu.VMEM((micro, C, T, R, CH), BF16),
@@ -589,7 +605,6 @@
             pltpu.VMEM((micro, C, R, CH), BF16),
             pltpu.VMEM((micro, C, T, R, CH), BF16),
             pltpu.VMEM((micro, C, T, R, CH), BF16),
-            pltpu.VMEM((micro, C, TOK, 2 * F), BF16),
             pltpu.VMEM((micro, C, TOK, F), BF16),
             pltpu.VMEM((micro, C, TOK, F), BF16),
             pltpu.VMEM((micro, TOK, F), F32),
@@ -625,7 +640,7 @@
             flops=flops, bytes_accessed=24 * D * F // 2, transcendentals=micro * TOK * F
         ),
         compiler_params=pltpu.CompilerParams(
-            collective_id=0, has_side_effects=True, vmem_limit_bytes=46 * 1024 * 1024
+            collective_id=0, has_side_effects=True, vmem_limit_bytes=52 * 1024 * 1024
         ),
     )(lengths, section_inputs[0], gain, cotangent, w_gate[0], w_up[0], w_down[0])
     gate, up, down, gain_out, rows = pl.pallas_call(

time: 130 us -> 129 us (level)
    pallas_call x1, Pallas kernels: 127 us -> 126 us  [body(): pl.pallas_call(functools.partial(kernel, dims), out_shape=(pltpu.VMEM((F,...]
where the time goes in v5:
time: 129 us
  Pallas kernels  128 us (99%)
    pallas_call x1, Pallas kernels, body(): pl.pallas_call(functools.partial(kernel, dims), out_shape=(pltpu.VMEM((F,...  126 us

profile of v5, /device:TPU:0, one launch (start us, length us, event | category | flops | bytes accessed | tf_op | source)
XLA Modules:
  0.0 128.8 jit_solution(17007299321731115367)
XLA Ops:
  0.6 125.6 %shard_map.110 = (bf16[640,1024]{1,0:T(8,128)(2,1)S(1)}, f32[1,4096]{1,0:T(1,128)S(1)}, bf16[2,16,4096]{2,1,0:T(8,128)(2,1)S(1)}, f32[1024,1280]{1,0:T(8,128)S(1...) custom-call(s32[2,8]{1,0:T(2,128)} %len_ref.1, bf16[2,16,4096]{2,1,0:T(8,128)(2,1)} %bitcast.14, ...), custom_call_target="tpu_custom_call" | custom-call | flops 10737418240 | bytes 31457280 | tf_op jit(solution)/shard_map/pallas_call | solution.py:580
  126.2 2.4 %shard_map.111 = (bf16[1024,640]{1,0:T(8,128)(2,1)}, bf16[1024,640]{1,0:T(8,128)(2,1)}, bf16[640,1024]{1,0:T(8,128)(2,1)}, f32[1,4096]{1,0:T(1,128)}, bf16[2,16,4096]{2,1,0:T(8,128)(2,1)}) custom-call(bf16[640,1024]{1,0:T(8,128)(2,1)S(1)} %get-tuple-element.16.down, f32[1,4096]{1,0:T(1,128)S(1)} %get-tuple-element.17.gain, ...), custom_call_target="tpu_custom_call" | custom-call | tf_op jit(solution)/shard_map/pallas_call | solution.py:646

commit v6 on v5

--- a/solution.py
+++ b/solution.py
@@ -349,9 +349,7 @@
                 def _():
                     spread_row(ubuf, 1, c, s_u, r_u)
             grad_hidden += dot(rows_of(ubuf, m, c), wdt[c * CH : (c + 1) * CH, :], NN)
-        exchange_slices(ubuf, uslice, 1, m)
         hgrad[m, d] = grad_hidden.astype(BF16)
-        exchange_all(hgrad, 3, m)
         both = jnp.concatenate(
             [(grad_hidden * ups[m]).astype(BF16), (grad_hidden * act[m]).astype(BF16)], axis=1
         )
@@ -362,6 +360,9 @@
             for k in range(1, T):
                 j = tpeer(k)
                 send(pbuf.at[m, c, j], rbuf.at[m, c, t], s_p.at[m, c], r_p.at[m, c], {"tensor": j})
+            if c == 0:
+                exchange_slices(ubuf, uslice, 1, m)
+                exchange_all(hgrad, 3, m)
     def send_gain():
         for k in range(1, T):
             send(gsum, gten.at[t], s_gain.at[0], r_gain.at[0], {"tensor": tpeer(k)})

time: 129 us -> 129 us (level)
  no operation moved by 1% of the time
where the time goes in v6:
time: 129 us
  Pallas kernels  128 us (99%)
    pallas_call x1, Pallas kernels, body(): pl.pallas_call(functools.partial(kernel, dims), out_shape=(pltpu.VMEM((F,...  125 us

profile of v6, /device:TPU:0, one launch (start us, length us, event | category | flops | bytes accessed | tf_op | source)
XLA Modules:
  0.0 128.6 jit_solution(9342537390971401680)
XLA Ops:
  0.6 125.4 %shard_map.110 = (bf16[640,1024]{1,0:T(8,128)(2,1)S(1)}, f32[1,4096]{1,0:T(1,128)S(1)}, bf16[2,16,4096]{2,1,0:T(8,128)(2,1)S(1)}, f32[1024,1280]{1,0:T(8,128)S(1...) custom-call(s32[2,8]{1,0:T(2,128)} %len_ref.1, bf16[2,16,4096]{2,1,0:T(8,128)(2,1)} %bitcast.14, ...), custom_call_target="tpu_custom_call" | custom-call | flops 10737418240 | bytes 31457280 | tf_op jit(solution)/shard_map/pallas_call | solution.py:581
  126.1 2.4 %shard_map.111 = (bf16[1024,640]{1,0:T(8,128)(2,1)}, bf16[1024,640]{1,0:T(8,128)(2,1)}, bf16[640,1024]{1,0:T(8,128)(2,1)}, f32[1,4096]{1,0:T(1,128)}, bf16[2,16,4096]{2,1,0:T(8,128)(2,1)}) custom-call(bf16[640,1024]{1,0:T(8,128)(2,1)S(1)} %get-tuple-element.16.down, f32[1,4096]{1,0:T(1,128)S(1)} %get-tuple-element.17.gain, ...), custom_call_target="tpu_custom_call" | custom-call | tf_op jit(solution)/shard_map/pallas_call | solution.py:647
